TPU v7x, 256 devices: a whole 4x4x8 slice. The times are simulated.
256 devices in a mesh: grp: 2 (over core), beam: 16 (over z, x_lo), tp: 8 (over x_hi, y).
Axes of the slice: x: 4 (x_hi: 2, x_lo: 2; x = x_hi * 2 + x_lo), y: 4, z: 8, core: 2. Of those that a mesh axis runs over, the one named last changes fastest.
Arguments:
- queries: bfloat16 [2, 1024, 4, 8192], P('grp', 'beam', None, 'tp'), may hold values from -128 to 128
- new_kv: bfloat16 [2, 1024, 4, 2048], P('grp', 'beam', None, 'tp'), may hold values from -12 to 12
- prompt_key_value: bfloat16 [2, 2, 4096, 2048], P('grp', None, 'beam', 'tp'), may hold values from -12 to 12
- step_key_value: bfloat16 [2, 1024, 128, 2048], P('grp', 'beam', None, 'tp'), may hold values from -12 to 12
- parent_dev: int32 [1024, 1], replicated, may hold values from 0 to 15; in each aligned block of 64 rows (0 to 63, 64 to 127, ...) at most 8 rows name the same one
- parent_slot: int32 [1024], replicated, may hold values from 0 to 63
- cache_len: int32 [1024], replicated, may hold values from 1 to 128, as said below
- prompt_ids: int32 [1024], P('beam'), may hold values from 0 to 1
- score_weights: float32 [2, 8192], P('grp', 'tp'), may hold values from -0.0625 to 0.0625
Outputs:
- attended: bfloat16 [2, 1024, 4, 8192], P('grp', 'beam', None, 'tp')
- beam_score: float32 [1024], P('beam')
Inputs may be any that keep to these rules, and one draw needn't show every extreme that they name: `parent_dev`: among the 64 beams of one device, at most 8 have parents on one device, and this bound is reached. `cache_len`: each device's block of 64 beams holds at least one beam of length 128.
All inputs are finite; a program needn't handle non-finite values.
Results may differ from a plain program's by a relative error of at most 0.0065.
Values may be sent and summed in bfloat16 or wider, within the bound.
A program may use at most 128 MiB of HBM per device.

v0:
```python
import math

import jax
import jax.numpy as jnp
from jax import lax
from jax.sharding import PartitionSpec as P

HEAD_SIZE = 128


floor_score = -1e30


def flash_block(partial_value, query_five, key_matrix, value_matrix, row_visible):
    summed, highest, weight_sum = partial_value
    scale = 1.0 / math.sqrt(query_five.shape[-1])
    scores = (
        jnp.einsum("brgjd,kgd->brgjk", query_five, key_matrix, preferred_element_type=jnp.float32)
        * scale
    )
    visible = row_visible[:, None, None, None, None]
    scores = jnp.where(visible, scores, floor_score)
    raised = jnp.maximum(highest, jnp.max(scores, axis=-1))
    weights = jnp.where(visible, jnp.exp(scores - raised[..., None]), 0.0)
    shrink = jnp.exp(highest - raised)
    weight_sum = weight_sum * shrink + jnp.sum(weights, axis=-1)
    summed = summed * shrink[..., None] + jnp.einsum(
        "brgjk,kgd->brgjd",
        weights,
        value_matrix.astype(jnp.float32),
        precision=lax.Precision.HIGHEST,
    )
    return (summed, raised, weight_sum)


def cache_part(query_five, page_rows, lengths):
    count_beams, positions = (page_rows.shape[0], page_rows.shape[1])
    kv_heads = query_five.shape[2]
    scale = 1.0 / math.sqrt(HEAD_SIZE)
    halves = page_rows.reshape(count_beams, positions, kv_heads, 2, HEAD_SIZE)
    scores = (
        jnp.einsum(
            "brgjd,bkgd->brgjk", query_five, halves[:, :, :, 0], preferred_element_type=jnp.float32
        )
        * scale
    )
    visible = (jnp.arange(positions)[None, :] < lengths[:, None])[:, None, None, None, :]
    scores = jnp.where(visible, scores, floor_score)
    highest = jnp.max(scores, axis=-1)
    weights = jnp.where(visible, jnp.exp(scores - highest[..., None]), 0.0)
    weight_sum = jnp.sum(weights, axis=-1)
    summed = jnp.einsum(
        "brgjk,bkgd->brgjd",
        weights,
        halves[:, :, :, 1].astype(jnp.float32),
        precision=lax.Precision.HIGHEST,
    )
    return (summed, highest, weight_sum)


def own_part(query_five, own_rows):
    count_beams, tokens = (own_rows.shape[0], own_rows.shape[1])
    kv_heads = query_five.shape[2]
    scale = 1.0 / math.sqrt(HEAD_SIZE)
    halves = own_rows.reshape(count_beams, tokens, kv_heads, 2, HEAD_SIZE)
    scores = (
        jnp.einsum(
            "brgjd,btgd->brgjt", query_five, halves[:, :, :, 0], preferred_element_type=jnp.float32
        )
        * scale
    )
    visible = (jnp.arange(tokens)[None, :] <= jnp.arange(tokens)[:, None])[None, :, None, None, :]
    scores = jnp.where(visible, scores, floor_score)
    highest = jnp.max(scores, axis=-1)
    weights = jnp.where(visible, jnp.exp(scores - highest[..., None]), 0.0)
    weight_sum = jnp.sum(weights, axis=-1)
    summed = jnp.einsum(
        "brgjt,btgd->brgjd",
        weights,
        halves[:, :, :, 1].astype(jnp.float32),
        precision=lax.Precision.HIGHEST,
    )
    return (summed, highest, weight_sum)


def combine(members):
    highest = members[0][1]
    for member in members[1:]:
        highest = jnp.maximum(highest, member[1])
    summed = jnp.zeros_like(members[0][0])
    weight_sum = jnp.zeros_like(members[0][2])
    for member in members:
        factor = jnp.exp(member[1] - highest)
        summed = summed + member[0] * factor[..., None]
        weight_sum = weight_sum + member[2] * factor
    return summed / weight_sum[..., None]


def on_device(
    queries,
    new_kv,
    prompt_key_value,
    step_key_value,
    parent_dev,
    parent_slot,
    cache_len,
    prompt_ids,
    score_weights,
):
    holders = lax.axis_size("beam")
    holder_idx = lax.axis_index("beam")
    beams_here = queries.shape[1]
    decoded = queries.shape[2]
    kv_heads = new_kv.shape[3] // (2 * HEAD_SIZE)
    queries_per_group = queries.shape[3] // (kv_heads * HEAD_SIZE)
    capacity = max(2, 2 * beams_here // holders)
    prompts = prompt_key_value.shape[1]
    query_five = queries[0].reshape(beams_here, decoded, kv_heads, queries_per_group, HEAD_SIZE)
    lengths_all = cache_len.reshape(holders, beams_here)
    my_lengths = lax.dynamic_index_in_dim(lengths_all, holder_idx, 0, keepdims=False)
    parents = parent_dev[:, 0].reshape(holders, beams_here)
    parent_slots = parent_slot.reshape(holders, beams_here)
    matches = (parents[:, :, None] == jnp.arange(holders)[None, None, :]).astype(jnp.int32)
    before = jnp.cumsum(matches, axis=1) - matches
    rank_of = jnp.sum(before * matches, axis=2)
    my_parents = lax.dynamic_index_in_dim(parents, holder_idx, 0, keepdims=False)
    my_ranks = lax.dynamic_index_in_dim(rank_of, holder_idx, 0, keepdims=False)
    arrival = my_parents * capacity + my_ranks
    served = (parents == holder_idx)[:, :, None] & (
        rank_of[:, :, None] == jnp.arange(capacity)[None, None, :]
    )
    served_slot = jnp.sum(jnp.where(served, parent_slots[:, :, None], 0), axis=1)
    local_pages = step_key_value[0]
    outgoing = jnp.take(local_pages, served_slot.reshape(-1), axis=0).reshape(
        (holders, capacity) + local_pages.shape[1:]
    )
    incoming = lax.all_to_all(outgoing, "beam", split_axis=0, concat_axis=0, tiled=True)
    child_pages = jnp.take(
        incoming.reshape((holders * capacity,) + local_pages.shape[1:]), arrival, axis=0
    )
    cache_terms = cache_part(query_five, child_pages, my_lengths)
    row_shape = (beams_here, decoded, kv_heads, queries_per_group)
    initial = (
        jnp.zeros(row_shape + (HEAD_SIZE,), jnp.float32),
        jnp.full(row_shape, floor_score, jnp.float32),
        jnp.zeros(row_shape, jnp.float32),
    )
    segment = lax.all_gather(prompt_key_value, "beam", axis=2, tiled=True)
    length = segment.shape[2]
    block_len = math.gcd(length, 512)

    def advance(position, running):
        window = lax.dynamic_slice_in_dim(segment[0], position * block_len, block_len, 1)
        window = window.reshape(prompts, block_len, kv_heads, 2, HEAD_SIZE)
        for member in range(prompts):
            running = flash_block(
                running,
                query_five,
                window[member, :, :, 0],
                window[member, :, :, 1],
                prompt_ids == member,
            )
        return running

    prompt_terms = lax.fori_loop(0, length // block_len, advance, initial)
    own_terms = own_part(query_five, new_kv[0])
    result = combine([prompt_terms, cache_terms, own_terms])
    attended = result.reshape(
        1, beams_here, decoded, kv_heads * queries_per_group * HEAD_SIZE
    ).astype(jnp.bfloat16)
    share = (
        jnp.sum(attended[0].astype(jnp.float32) * score_weights[0][None, None, :], axis=(1, 2))
        / decoded
    )
    beam_score = lax.psum(share, ("grp", "tp"))
    return (attended, beam_score)


def solution(mesh):
    in_specs = (
        P("grp", "beam", None, "tp"),
        P("grp", "beam", None, "tp"),
        P("grp", None, "beam", "tp"),
        P("grp", "beam", None, "tp"),
        P(),
        P(),
        P(),
        P("beam"),
        P("grp", "tp"),
    )
    out_specs = (P("grp", "beam", None, "tp"), P("beam"))
    return jax.shard_map(
        on_device, mesh=mesh, in_specs=in_specs, out_specs=out_specs, check_vma=False
    )
```

profile of v0, /device:TPU:1, one launch (start us, length us, event | category | flops | bytes accessed | tf_op | source)
XLA Modules:
  0.0 496.0 jit_solution(2548063621711286279)
XLA Ops:
  7.2 1.8 copy.99
  11.8 1.4 select_reduce_fusion
  13.8 8.6 %gather_fusion = bf16[128,128,256]{2,1,0:T(8,128)(2,1)} fusion(bf16[64,128,256]{2,1,0:T(8,128)(2,1)} %bitcast.409, s32[1024]{0:T(1024)S(1)} %pad_clamp_fusion.1), kind=kCustom, calls=%fused_computation | custom fusion | bytes 16777728 | tf_op jit(solution)/shard_map/jit(_take)/gather | solution.py:134
  22.4 7.4 %broadcast_select_fusion = bf16[16,8,128,256]{3,2,1,0:T(8,128)(2,1)} fusion(bf16[16,8,128,256]{3,2,1,0:T(8,128)(2,1)} %bitcast.404, pred[16,8]{1,0:T(8,128)(4,1)S(1)} %compare_and_fusion), kind=kLoop, calls=%fused_computation.63 | loop fusion | flops 4194304 | bytes 16777344 | tf_op jit(solution)/shard_map/jit(_take)/select_n | solution.py:134
  29.8 10.2 %all-to-all-start = ((bf16[16,8,128,256]{3,2,1,0:T(8,128)(2,1)}), bf16[16,8,128,256]{3,2,1,0:T(8,128)(2,1)}, u32[]{:S(2)}, u32[]{:S(2)}) async-start(bf16[16,8,128,256]{3,2,1,0:T(8,128)(2,1)} %broadcast_select_fusion), calls=%async_computation | async-start | bytes 16777216 | tf_op jit(solution)/shard_map/all_to_all | solution.py:137
  41.3 2.4 fusion.99
  44.4 232.2 %all-gather.2.cloned.1.call-done = bf16[1,2,4096,256]{2,3,1,0:T(8,128)(2,1)} async-done(((bf16[1,2,256,256]{2,3,1,0:T(8,128)(2,1)}), bf16[1,2,4096,256]{2,3,1,0:T(8,128)(2,1)}) %all-gather.2.cloned.1.call-update) | async-done | bytes 4194320 | tf_op jit(solution)/shard_map/all_gather | solution.py:148
  276.6 141.6 %while.18 = (s32[]{:T(128)}, f32[64,4,1,8,128]{4,0,3,1,2:T(8,128)}, f32[64,4,1,8]{0,3,1,2:T(8,128)S(1)}, f32[64,4,1,8]{0,3,1,2:T(8,128)S(1)}, s32[64]{0:T(128)S(...) while((s32[]{:T(128)}, f32[64,4,1,8,128]{4,0,3,1,2:T(8,128)}, ...), condition=%wide.region_5.6_spmd.clone, body=%wide.region_0.5_spmd.clone.sunk | while | flops 3784591360 | bytes 49016524 | solution.py:165
  277.6 2.7 bitcast_reduce_fusion.4
  281.1 1.4 copy-done
  282.5 4.2 fusion.114
  286.7 4.0 fusion.115
  290.7 2.6 fusion.116
  294.4 2.7 bitcast_reduce_fusion.4
  299.3 5.2 %fusion.114 = f32[64,4,1,8,128]{4,0,3,1,2:T(8,128)S(1)} fusion(f32[512,64,4,8]{0,1,3,2:T(8,128)S(1)} %copy-done, f32[64,4,8]{0,2,1:T(8,128)S(1)} %bitcast.411, pred[64]{0:T(512)(128)(4,1)S(1)} %get-tuple-element.283, f32[64,4,1,8,128]{4,0,3,1,2:T(8,128)} %get-tuple-element.307, f32[64,4,8]{0,2,1:T(8,128)S(1)} %get-tuple-element.289, ...), kind=kOutput, calls=%fused_computation.34.clone.1 | convolution fusion | flops 1615855616 | bytes 6472705 | tf_op jit(solution)/shard_map/while/body/eval_jaxpr/brgjk,kgd->brgjd/dot_general | solution.py:27
  304.5 4.0 fusion.115
  308.5 2.6 fusion.116
  312.3 2.7 bitcast_reduce_fusion.4
  317.1 5.2 %fusion.114 = f32[64,4,1,8,128]{4,0,3,1,2:T(8,128)S(1)} fusion(f32[512,64,4,8]{0,1,3,2:T(8,128)S(1)} %copy-done, f32[64,4,8]{0,2,1:T(8,128)S(1)} %bitcast.411, pred[64]{0:T(512)(128)(4,1)S(1)} %get-tuple-element.283, f32[64,4,1,8,128]{4,0,3,1,2:T(8,128)} %get-tuple-element.307, f32[64,4,8]{0,2,1:T(8,128)S(1)} %get-tuple-element.289, ...), kind=kOutput, calls=%fused_computation.34.clone.1 | convolution fusion | flops 1615855616 | bytes 6472705 | tf_op jit(solution)/shard_map/while/body/eval_jaxpr/brgjk,kgd->brgjd/dot_general | solution.py:27
  322.3 4.0 fusion.115
  326.4 2.6 fusion.116
  330.1 2.7 bitcast_reduce_fusion.4
  334.9 5.2 %fusion.114 = f32[64,4,1,8,128]{4,0,3,1,2:T(8,128)S(1)} fusion(f32[512,64,4,8]{0,1,3,2:T(8,128)S(1)} %copy-done, f32[64,4,8]{0,2,1:T(8,128)S(1)} %bitcast.411, pred[64]{0:T(512)(128)(4,1)S(1)} %get-tuple-element.283, f32[64,4,1,8,128]{4,0,3,1,2:T(8,128)} %get-tuple-element.307, f32[64,4,8]{0,2,1:T(8,128)S(1)} %get-tuple-element.289, ...), kind=kOutput, calls=%fused_computation.34.clone.1 | convolution fusion | flops 1615855616 | bytes 6472705 | tf_op jit(solution)/shard_map/while/body/eval_jaxpr/brgjk,kgd->brgjd/dot_general | solution.py:27
  340.2 4.0 fusion.115
  344.2 2.6 fusion.116
  347.9 2.7 bitcast_reduce_fusion.4
  351.4 1.4 copy-done
  352.8 5.2 %fusion.114 = f32[64,4,1,8,128]{4,0,3,1,2:T(8,128)S(1)} fusion(f32[512,64,4,8]{0,1,3,2:T(8,128)S(1)} %copy-done, f32[64,4,8]{0,2,1:T(8,128)S(1)} %bitcast.411, pred[64]{0:T(512)(128)(4,1)S(1)} %get-tuple-element.283, f32[64,4,1,8,128]{4,0,3,1,2:T(8,128)} %get-tuple-element.307, f32[64,4,8]{0,2,1:T(8,128)S(1)} %get-tuple-element.289, ...), kind=kOutput, calls=%fused_computation.34.clone.1 | convolution fusion | flops 1615855616 | bytes 6472705 | tf_op jit(solution)/shard_map/while/body/eval_jaxpr/brgjk,kgd->brgjd/dot_general | solution.py:27
  358.0 4.0 fusion.115
  362.0 2.6 fusion.116
  365.7 2.7 bitcast_reduce_fusion.4
  370.6 5.2 %fusion.114 = f32[64,4,1,8,128]{4,0,3,1,2:T(8,128)S(1)} fusion(f32[512,64,4,8]{0,1,3,2:T(8,128)S(1)} %copy-done, f32[64,4,8]{0,2,1:T(8,128)S(1)} %bitcast.411, pred[64]{0:T(512)(128)(4,1)S(1)} %get-tuple-element.283, f32[64,4,1,8,128]{4,0,3,1,2:T(8,128)} %get-tuple-element.307, f32[64,4,8]{0,2,1:T(8,128)S(1)} %get-tuple-element.289, ...), kind=kOutput, calls=%fused_computation.34.clone.1 | convolution fusion | flops 1615855616 | bytes 6472705 | tf_op jit(solution)/shard_map/while/body/eval_jaxpr/brgjk,kgd->brgjd/dot_general | solution.py:27
  375.8 4.0 fusion.115
  379.9 2.6 fusion.116
  383.6 2.7 bitcast_reduce_fusion.4
  388.4 5.2 %fusion.114 = f32[64,4,1,8,128]{4,0,3,1,2:T(8,128)S(1)} fusion(f32[512,64,4,8]{0,1,3,2:T(8,128)S(1)} %copy-done, f32[64,4,8]{0,2,1:T(8,128)S(1)} %bitcast.411, pred[64]{0:T(512)(128)(4,1)S(1)} %get-tuple-element.283, f32[64,4,1,8,128]{4,0,3,1,2:T(8,128)} %get-tuple-element.307, f32[64,4,8]{0,2,1:T(8,128)S(1)} %get-tuple-element.289, ...), kind=kOutput, calls=%fused_computation.34.clone.1 | convolution fusion | flops 1615855616 | bytes 6472705 | tf_op jit(solution)/shard_map/while/body/eval_jaxpr/brgjk,kgd->brgjd/dot_general | solution.py:27
  393.7 4.0 fusion.115
  397.7 2.6 fusion.116
  401.4 2.7 bitcast_reduce_fusion.4
  406.3 5.2 %fusion.114 = f32[64,4,1,8,128]{4,0,3,1,2:T(8,128)S(1)} fusion(f32[512,64,4,8]{0,1,3,2:T(8,128)S(1)} %copy-done, f32[64,4,8]{0,2,1:T(8,128)S(1)} %bitcast.411, pred[64]{0:T(512)(128)(4,1)S(1)} %get-tuple-element.283, f32[64,4,1,8,128]{4,0,3,1,2:T(8,128)} %get-tuple-element.307, f32[64,4,8]{0,2,1:T(8,128)S(1)} %get-tuple-element.289, ...), kind=kOutput, calls=%fused_computation.34.clone.1 | convolution fusion | flops 1615855616 | bytes 6472705 | tf_op jit(solution)/shard_map/while/body/eval_jaxpr/brgjk,kgd->brgjd/dot_general | solution.py:27
  411.5 4.0 fusion.115
  415.5 2.6 fusion.116
  418.4 6.2 %gather_fusion.1 = bf16[64,128,256]{2,1,0:T(8,128)(2,1)} fusion(bf16[128,128,256]{2,1,0:T(8,128)(2,1)} %bitcast.4, s32[1024]{0:T(1024)S(1)} %pad_clamp_fusion), kind=kCustom, calls=%fused_computation.1 | custom fusion | bytes 8388864 | tf_op jit(solution)/shard_map/jit(_take)/gather | solution.py:138
  424.5 6.4 %copy.105 = bf16[64,128,256]{1,2,0:T(8,128)(2,1)} copy(bf16[64,128,256]{2,1,0:T(8,128)(2,1)} %gather_fusion.1) | data formatting | bytes 8388608 | tf_op jit(solution)/shard_map/jit(_take)/gather | solution.py:138
  430.9 6.4 %copy.106 = bf16[64,128,1,2,128]{4,1,0,3,2:T(8,128)(2,1)} copy(bf16[64,128,1,2,128]{1,4,3,0,2:T(8,128)(2,1)} %bitcast.410) | data formatting | bytes 8388608 | tf_op jit(solution)/shard_map/jit(_take)/gather | solution.py:138
  437.3 2.6 broadcast_select_fusion.1
  443.6 3.6 multiply_reduce_fusion
  448.1 41.1 %psum.7 = f32[64]{0:T(128)} all-reduce(f32[64]{0:T(128)S(1)} %broadcast_multiply_fusion), channel_id=1, replica_groups=mesh['grp'=2,'beam'=16,'tp'=8] {'grp','tp'}, use_global_device_ids=true, to_apply=%region_14.15 | all-reduce | flops 64 | bytes 512 | tf_op jit(solution)/shard_map/psum | solution.py:175
  (122 shorter events, 33.3 us)
Async XLA Ops:
  7.2 269.4 %all-gather.2.cloned.1.call-start = ((), (), s32[]{:S(2)}) async-start(), calls=%async_computation.1 | async-start | bytes 4456448 | tf_op jit(solution)/shard_map/all_gather | solution.py:148
  29.8 10.3 %copy-start.1 = (bf16[1,64,4,1024]{3,2,1,0:T(4,128)(2,1)S(1)}, bf16[1,64,4,1024]{3,2,1,0:T(4,128)(2,1)}, u32[]{:S(2)}) copy-start(bf16[1,64,4,1024]{3,2,1,0:T(4,128)(2,1)} %param.11) | copy-start | bytes 1572868
  29.8 10.9 %copy-start.2 = (bf16[1,64,4,256]{3,2,1,0:T(4,128)(2,1)S(1)}, bf16[1,64,4,256]{3,2,1,0:T(4,128)(2,1)}, u32[]{:S(2)}) copy-start(bf16[1,64,4,256]{3,2,1,0:T(4,128)(2,1)} %param.12) | copy-start | bytes 393220
  29.8 11.0 %copy-start.3 = (s32[1024]{0:T(1024)S(1)}, s32[1024]{0:T(1024)}, u32[]{:S(2)}) copy-start(s32[1024]{0:T(1024)} %param.17) | copy-start | bytes 12292
  29.8 388.5 %all-to-all-start = ((bf16[16,8,128,256]{3,2,1,0:T(8,128)(2,1)}), bf16[16,8,128,256]{3,2,1,0:T(8,128)(2,1)}, u32[]{:S(2)}, u32[]{:S(2)}) async-start(bf16[16,8,128,256]{3,2,1,0:T(8,128)(2,1)} %broadcast_select_fusion), calls=%async_computation | async-start | bytes 16777216 | tf_op jit(solution)/shard_map/all_to_all | solution.py:137
  40.1 236.5 %copy-start.5 = (s32[64]{0:T(128)S(1)}, s32[64]{0:T(128)}, u32[]{:S(2)}) copy-start(s32[64]{0:T(128)} %param.18) | copy-start | bytes 772
  280.3 2.2 copy-start
  297.1 2.2 copy-start
  314.9 2.2 copy-start
  332.8 2.2 copy-start
  350.6 2.2 copy-start
  368.4 2.2 copy-start
  386.2 2.2 copy-start
  404.1 2.2 copy-start
  441.3 2.2 copy-start.4
  441.3 2.2 copy-start.6
Sparse Core Ops, SparseCore 0:
  10.3 266.2 all-gather.1
where the time goes:
time: 500 us; the launch traced here: 496 us
  waiting for transfers between devices  232 us (46%)
  matrix products  109 us (22%)
  local copies, waits for them, and re-layouts  52.7 us (11%)
  blocking collectives  41.1 us (8%)
  other arithmetic  35.8 us (7%)
  between operations  14.3 us (3%)
  starting transfers between devices  10.3 us (2%)
    all_gather x1, waiting for transfers between devices, on_device(): segment = lax.all_gather(prompt_key_value, 'beam', axis=2, tiled=True)  232 us
    dot_general x16, matrix products, flash_block(): jnp.einsum('brgjk,kgd->brgjd', weights, value_matrix.astype(jnp.float32),...  72.9 us
    psum x1, blocking collectives, on_device(): beam_score = lax.psum(share, ('grp', 'tp'))  41.1 us
    dot_general x16, matrix products, flash_block(): jnp.einsum('brgjd,kgd->brgjk', query_five, key_matrix, preferred_element_...  27.5 us
    reduce_sum x8, other arithmetic, flash_block(): weight_sum = weight_sum * shrink + jnp.sum(weights, axis=-1)  20.5 us
    gather x3, local copies, waits for them, and re-layouts, on_device(): jnp.take(incoming.reshape((holders * capacity,) + local_pages.shape[1:]),...  18.9 us
    while x24, local copies, waits for them, and re-layouts  11.1 us
    all_to_all x1, starting transfers between devices, on_device(): lax.all_to_all(outgoing, 'beam', split_axis=0, concat_axis=0, tiled=True)  10.2 us
  transfers between devices with their start and end apart: 2, of which 1 were waited for; matrix products, arithmetic and copies ran while one was open for 31% of the time, Pallas kernels for 0%

commit v1 on v0

v1 whole, which is shorter than its diff:
```python
import functools
import math

import jax
import jax.numpy as jnp
from jax import lax
from jax.experimental import pallas as pl
from jax.experimental.pallas import tpu as pltpu
from jax.sharding import PartitionSpec as P

MESH = pl.DeviceIdType.MESH
F32, BF16, I32 = jnp.float32, jnp.bfloat16, jnp.int32

HEAD = 128
BEAMS = 64
ROWS = 32
CAP = 8
HOLD = 16
TILE = 8
TILES = BEAMS // TILE + 1
PLACES = TILES * TILE
TROWS = TILE * ROWS
SHARD = 256
NEWPAD = 16
SCALE = math.log2(math.e) / math.sqrt(HEAD)
LOW = -1e30
TAB = HOLD + PLACES


def iota(shape, axis):
    return lax.broadcasted_iota(I32, shape, axis)


def table_kernel(meta_ref, pid_ref, tab_ref):
    me = lax.axis_index("beam")
    upper = (iota((BEAMS, BEAMS), 0) < iota((BEAMS, BEAMS), 1)).astype(F32)
    pdev = meta_ref[0]
    slot = meta_ref[1].astype(F32)
    length = meta_ref[2].astype(F32)
    lane = iota((HOLD, 128), 1)
    head = jnp.zeros((HOLD, 128), F32)

    served = (pdev == me).astype(F32)
    rank = jnp.dot(served, upper, preferred_element_type=F32)
    mine = meta_ref[0, pl.ds(me, 1), :]
    ahead = (mine - me + HOLD) & (HOLD - 1)
    row16 = iota((HOLD, BEAMS), 0)
    own = (jnp.broadcast_to(ahead, (HOLD, BEAMS)) == row16).astype(F32)
    own_rank = jnp.dot(own, upper, preferred_element_type=F32)
    beam = iota((HOLD, BEAMS), 1).astype(F32)
    for k in range(CAP):
        pick = jnp.where(rank == k, served, 0.0)
        head = jnp.where(lane == k, jnp.sum(pick * slot, axis=1, keepdims=True), head)
        head = jnp.where(lane == CAP + k, jnp.sum(pick * length, axis=1, keepdims=True), head)
        pick = jnp.where(own_rank == k, own, 0.0)
        head = jnp.where(lane == 2 * CAP + k, jnp.sum(pick * beam, axis=1, keepdims=True), head)
    tab_ref[0:HOLD, :] = head.astype(I32)

    arrival = jnp.sum(own * (row16.astype(F32) * CAP + own_rank), axis=0, keepdims=True)
    first = (pid_ref[...] == 0).astype(F32)
    before = jnp.dot(jnp.broadcast_to(first, (8, BEAMS)), upper, preferred_element_type=F32)[0:1]
    count = jnp.sum(first, axis=1, keepdims=True).astype(I32)
    filled = (count + (TILE - 1)) & (-TILE)
    after = filled.astype(F32) + iota((1, BEAMS), 1).astype(F32) - before
    place = jnp.where(first > 0.5, before, after)

    lane = iota((PLACES, 128), 1)
    beam = iota((PLACES, BEAMS), 1).astype(F32)
    here = iota((PLACES, BEAMS), 0).astype(F32)
    at_place = (jnp.broadcast_to(place, (PLACES, BEAMS)) == here).astype(F32)
    holder = jnp.sum(at_place * beam, axis=1, keepdims=True)
    on_diag = (beam == here).astype(F32)
    arrival_col = jnp.sum(on_diag * arrival, axis=1, keepdims=True)
    place_col = jnp.sum(on_diag * place, axis=1, keepdims=True)
    tile_start = iota((PLACES, 128), 0) * TILE
    which = (tile_start >= filled).astype(F32)
    body = jnp.where(lane == 0, holder, 0.0)
    body = jnp.where(lane == 1, which, body)
    body = jnp.where(lane == 2, arrival_col, body)
    body = jnp.where(lane == 3, place_col, body)
    tab_ref[HOLD:TAB, :] = body.astype(I32)


OWN, XOWN, ANTI, XANTI = 0, 1, 14, 15
FWD = {1: 2, 2: 6, 3: 10}
BWD = {1: 3, 2: 7, 3: 11}
XFWD = {1: 4, 2: 8, 3: 12}
XBWD = {1: 5, 2: 9, 3: 13}


def dot_nt(a, b):
    return lax.dot_general(a, b, (((1,), (1,)), ((), ())), preferred_element_type=F32)


def dot_nn(a, b):
    return lax.dot_general(a, b, (((1,), (0,)), ((), ())), preferred_element_type=F32)


def main_kernel(
    groups, lanes_tp, tab, q_ref, kvn_ref, w_ref, prompt_hbm, pages_hbm,
    out_ref, score_ref,
    pages, kv0, kv1, kv2, kv3, send, recv, ret_out, ret_in, stat_out, stat_in,
    qt, kvt, acc, high, part, share, shares,
    q_ss, q_rs, r_ss, r_rs, s_ss, s_rs, f_ss, f_rs, b_ss, b_rs, x_ss, x_rs, c_ss, c_rs, l_sem,
):
    me = lax.axis_index("beam")
    grp = lax.axis_index("grp")
    tp = lax.axis_index("tp")
    group = grp * lanes_tp + tp
    up = lax.rem(me + 2, HOLD)
    down = lax.rem(me + HOLD - 2, HOLD)
    side = me + 1 - 2 * lax.rem(me, 2)

    held = (kv0, kv1, kv2, kv3)

    def shard_at(slot):
        return held[slot // 4].at[slot % 4]

    load_prompt = pltpu.make_async_copy(prompt_hbm, shard_at(OWN), l_sem.at[0])
    load_pages = pltpu.make_async_copy(pages_hbm, pages, l_sem.at[1])
    load_prompt.start()
    load_pages.start()

    barrier = pltpu.get_barrier_semaphore()

    def greet_beam(o, _):
        pl.semaphore_signal(barrier, inc=1, device_id={"beam": lax.rem(me + o, HOLD)}, device_id_type=MESH)
        return 0

    lax.fori_loop(1, HOLD, greet_beam, 0)

    def group_peer(o):
        peer = lax.rem(group + o, groups)
        return {"grp": lax.div(peer, lanes_tp), "tp": lax.rem(peer, lanes_tp)}

    if groups > 1:
        def greet_group(o, _):
            pl.semaphore_signal(barrier, inc=1, device_id=group_peer(o), device_id_type=MESH)
            return 0

        lax.fori_loop(1, groups, greet_group, 0)

    def span(o):
        return pl.ds(o * CAP, CAP)

    def pack(o, into):
        for k in range(CAP):
            into[o * CAP + k] = q_ref[tab[o, 2 * CAP + k]]

    pack(0, recv)
    pl.semaphore_wait(barrier, HOLD - 1 + groups - 1)

    def query_copy(o):
        return pltpu.make_async_remote_copy(
            src_ref=send.at[span(o)], dst_ref=recv.at[span(o)], send_sem=q_ss.at[o], recv_sem=q_rs.at[o],
            device_id={"beam": lax.rem(me + o, HOLD)}, device_id_type=MESH)

    def send_query(o, _):
        pack(o, send)
        query_copy(o).start()
        return 0

    lax.fori_loop(1, HOLD, send_query, 0)

    def shard_copy(src, dst, to, ss, rs, half=None):
        a, b = shard_at(src), shard_at(dst)
        if half is not None:
            a, b = a.at[half], b.at[half]
        return pltpu.make_async_remote_copy(
            src_ref=a, dst_ref=b, send_sem=ss, recv_sem=rs, device_id={"beam": to}, device_id_type=MESH)

    def fwd_copy(s):
        src = OWN if s == 1 else FWD[s - 1]
        if s == 4:
            return shard_copy(src, ANTI, up, f_ss.at[s], f_rs.at[s], 0)
        return shard_copy(src, FWD[s], up, f_ss.at[s], f_rs.at[s])

    def bwd_copy(s):
        src = OWN if s == 1 else BWD[s - 1]
        if s == 4:
            return shard_copy(src, ANTI, down, b_ss.at[s], b_rs.at[s], 1)
        return shard_copy(src, BWD[s], down, b_ss.at[s], b_rs.at[s])

    x_plan = [(OWN, XOWN)]
    for s in (1, 2, 3):
        x_plan += [(FWD[s], XFWD[s]), (BWD[s], XBWD[s])]
    x_plan += [(ANTI, XANTI)]

    def x_copy(i):
        src, dst = x_plan[i]
        return shard_copy(src, dst, side, x_ss.at[i], x_rs.at[i])

    load_prompt.wait()
    fwd_copy(1).start()
    bwd_copy(1).start()
    x_copy(0).start()

    def ring_step(s):
        fwd_copy(s).wait_recv()
        if s < 4:
            fwd_copy(s + 1).start()
            x_copy(2 * s - 1).start()
        bwd_copy(s).wait_recv()
        if s < 4:
            bwd_copy(s + 1).start()
            x_copy(2 * s).start()
        else:
            x_copy(7).start()

    def fill_tile(t, _):
        for i in range(TILE):
            b = tab[HOLD + t * TILE + i, 0]
            qt[t * TILE + i] = q_ref[b]
            kvt[t * TILE + i] = kvn_ref[b]
        return 0

    lax.fori_loop(0, TILES, fill_tile, 0)

    def with_ones(values):
        return jnp.concatenate([values, jnp.ones(values.shape, BF16)], axis=1)

    diag = (iota((TROWS, 128), 0) & 127) == iota((TROWS, 128), 1)
    column = iota((ROWS, 128), 1)

    def step_part(o, into_out, into_stat):
        c = lax.rem(me - o + HOLD, HOLD)
        blocks = []
        values = []
        for j in range(CAP // 2):
            k0, k1 = 2 * j, 2 * j + 1
            page0, page1 = pages[tab[c, k0]], pages[tab[c, k1]]
            keys = jnp.concatenate([page0[:, :HEAD], page1[:, :HEAD]], axis=0)
            values.append(with_ones(jnp.concatenate([page0[:, HEAD:], page1[:, HEAD:]], axis=0)))
            queries = recv[pl.ds(o * CAP + k0, 2)].reshape(2 * ROWS, HEAD)
            s = dot_nt(queries, keys)
            blocks.append(jnp.where(column < tab[c, CAP + k0], s[:ROWS, :128] * SCALE, LOW))
            blocks.append(jnp.where(column < tab[c, CAP + k1], s[ROWS:, 128:] * SCALE, LOW))
        s = jnp.concatenate(blocks, axis=0)
        top = jnp.max(s, axis=1, keepdims=True)
        p = jnp.exp2(s - top).astype(BF16)
        zero = jnp.zeros((ROWS, 128), BF16)
        sums = []
        for j in range(CAP // 2):
            p0, p1 = p[2 * j * ROWS:(2 * j + 1) * ROWS], p[(2 * j + 1) * ROWS:(2 * j + 2) * ROWS]
            wide = jnp.concatenate(
                [jnp.concatenate([p0, zero], axis=1), jnp.concatenate([zero, p1], axis=1)], axis=0)
            sums.append(dot_nn(wide, values[j]))
        sums = jnp.concatenate(sums, axis=0)
        total = sums[:, HEAD:]
        into_out[span(o)] = (sums[:, :HEAD] / total).astype(BF16).reshape(CAP, ROWS, HEAD)
        level = top + jnp.log2(total)
        flat = jnp.sum(jnp.where(diag, level, 0.0).reshape(2, 128, 128), axis=1)
        into_stat[o] = jnp.concatenate([flat, jnp.zeros((6, 128), F32)], axis=0)

    def back_copy(o):
        to = {"beam": lax.rem(me - o + HOLD, HOLD)}
        return (
            pltpu.make_async_remote_copy(
                src_ref=ret_out.at[span(o)], dst_ref=ret_in.at[span(o)], send_sem=r_ss.at[o],
                recv_sem=r_rs.at[o], device_id=to, device_id_type=MESH),
            pltpu.make_async_remote_copy(
                src_ref=stat_out.at[o], dst_ref=stat_in.at[o], send_sem=s_ss.at[o],
                recv_sem=s_rs.at[o], device_id=to, device_id_type=MESH),
        )

    def serve(o, _):
        query_copy(o).wait_recv()
        step_part(o, ret_out, stat_out)
        for copy in back_copy(o):
            copy.start()
        return 0

    load_pages.wait()
    step_part(0, ret_in, stat_in)

    def new_part(t, _):
        q = qt[pl.ds(t * TILE, TILE)].reshape(TROWS, HEAD)
        kv = kvt[pl.ds(t * TILE, TILE)].reshape(TILE * NEWPAD, 2 * HEAD)
        row, col = iota((TROWS, TILE * NEWPAD), 0), iota((TROWS, TILE * NEWPAD), 1)
        seen = ((row >> 5) == (col >> 4)) & ((col & 15) <= ((row >> 3) & 3))
        s = jnp.where(seen, dot_nt(q, kv[:, :HEAD]) * SCALE, LOW)
        top = jnp.max(s, axis=1, keepdims=True)
        p = jnp.exp2(s - top).astype(BF16)
        acc[pl.ds(t * TILE, TILE)] = dot_nn(p, with_ones(kv[:, HEAD:])).reshape(TILE, ROWS, 2 * HEAD)
        high[pl.ds(t * TILE, TILE)] = jnp.broadcast_to(top, (TROWS, 128)).reshape(TILE, ROWS, 128)
        return 0

    lax.fori_loop(0, TILES, new_part, 0)

    lax.fori_loop(1, 5, serve, 0)
    ring_step(1)
    lax.fori_loop(5, 9, serve, 0)
    ring_step(2)
    lax.fori_loop(9, 13, serve, 0)
    ring_step(3)
    lax.fori_loop(13, 16, serve, 0)

    def prompt_part(number):
        def one(t, _):
            own = tab[HOLD + t, 1]
            q = qt[pl.ds(t * TILE, TILE)].reshape(TROWS, HEAD)
            kv = held[number][:, own].reshape(4 * SHARD, 2 * HEAD)
            s = dot_nt(q, kv[:, :HEAD]) * SCALE
            old = high[pl.ds(t * TILE, TILE)].reshape(TROWS, 128)
            top = jnp.maximum(old, jnp.max(s, axis=1, keepdims=True))
            p = jnp.exp2(s - top[:, :1]).astype(BF16)
            fade = jnp.exp2(old - top)
            add = dot_nn(p, with_ones(kv[:, HEAD:]))
            was = acc[pl.ds(t * TILE, TILE)].reshape(TROWS, 2 * HEAD)
            new = was * jnp.concatenate([fade, fade], axis=1) + add
            acc[pl.ds(t * TILE, TILE)] = new.reshape(TILE, ROWS, 2 * HEAD)
            high[pl.ds(t * TILE, TILE)] = top.reshape(TILE, ROWS, 128)
            return 0

        lax.fori_loop(0, TILES, one, 0)

    x_copy(0).wait_recv()
    prompt_part(0)
    ring_step(4)
    for i in (1, 2):
        x_copy(i).wait_recv()
    prompt_part(1)
    for i in (3, 4):
        x_copy(i).wait_recv()
    prompt_part(2)
    for i in (5, 6, 7):
        x_copy(i).wait_recv()
    prompt_part(3)

    def await_back(o, _):
        for copy in back_copy(o):
            copy.wait_recv()
        return 0

    lax.fori_loop(1, HOLD, await_back, 0)

    lane_of = iota((ROWS, 128), 1) - iota((ROWS, 128), 0)

    def finish(i, _):
        for u in range(4):
            b = i * 4 + u
            a = tab[HOLD + b, 2]
            place = tab[HOLD + b, 3]
            line = stat_in[a >> 3, pl.ds((a >> 2) & 1, 1), :]
            level = jnp.sum(jnp.where(lane_of == (a & 3) * ROWS, line, 0.0), axis=1, keepdims=True)
            old = high[place]
            top = jnp.maximum(old, level)
            mine, theirs = jnp.exp2(old - top), jnp.exp2(level - top)
            sums = acc[place]
            whole = sums[:, :HEAD] * mine + ret_in[a].astype(F32) * theirs
            result = (whole / (sums[:, HEAD:] * mine + theirs)).astype(BF16)
            out_ref[b] = result
            part[pl.ds(b, 1), :] = jnp.sum(result.astype(F32) * w_ref[...], axis=0, keepdims=True)
        return 0

    lax.fori_loop(0, BEAMS // 4, finish, 0)

    score = jnp.sum(part[...], axis=1, keepdims=True)
    spot = iota((BEAMS, 128), 0) == iota((BEAMS, 128), 1)
    line = jnp.sum(jnp.where(spot, score, 0.0), axis=0, keepdims=True) * 0.25
    share[...] = jnp.broadcast_to(line, (8, 128))
    if groups > 1:
        def share_copy(o):
            return pltpu.make_async_remote_copy(
                src_ref=share, dst_ref=shares.at[group], send_sem=c_ss.at[o], recv_sem=c_rs.at[o],
                device_id=group_peer(o), device_id_type=MESH)

        def send_share(o, _):
            share_copy(o).start()
            return 0

        lax.fori_loop(1, groups, send_share, 0)
        shares[group] = share[...]

        def await_share(o, _):
            share_copy(o).wait()
            return 0

        lax.fori_loop(1, groups, await_share, 0)
        score_ref[...] = jnp.sum(shares[...], axis=0)
    else:
        score_ref[...] = share[...]

    def await_sends(o, _):
        query_copy(o).wait_send()
        for copy in back_copy(o):
            copy.wait_send()
        return 0

    lax.fori_loop(1, HOLD, await_sends, 0)
    for s in (1, 2, 3, 4):
        fwd_copy(s).wait_send()
        bwd_copy(s).wait_send()
    for i in range(8):
        x_copy(i).wait_send()


def on_device(queries, new_kv, prompt_key_value, step_key_value, parent_dev, parent_slot, cache_len, prompt_ids, score_weights):
    lanes_tp = lax.axis_size("tp")
    groups = lax.axis_size("grp") * lanes_tp
    meta = jnp.stack([parent_dev[:, 0], parent_slot, cache_len]).reshape(3, HOLD, BEAMS)
    vmem = pl.BlockSpec(memory_space=pltpu.VMEM)
    smem = pl.BlockSpec(memory_space=pltpu.SMEM)
    anywhere = pl.BlockSpec(memory_space=pl.ANY)
    table = pl.pallas_call(
        table_kernel,
        out_shape=jax.ShapeDtypeStruct((TAB, 128), I32),
        in_specs=[vmem, vmem],
        out_specs=vmem,
    )(meta, prompt_ids.reshape(1, BEAMS))
    q = queries.reshape(BEAMS, ROWS, HEAD)
    kvn = jnp.pad(new_kv[0], ((0, 0), (0, NEWPAD - new_kv.shape[2]), (0, 0)))
    weights = jnp.tile(score_weights.reshape(8, HEAD), (4, 1))
    dma = pltpu.SemaphoreType.DMA
    attended, score = pl.pallas_call(
        functools.partial(main_kernel, groups, lanes_tp),
        out_shape=(
            jax.ShapeDtypeStruct((BEAMS, ROWS, HEAD), BF16),
            jax.ShapeDtypeStruct((8, 128), F32),
        ),
        in_specs=[smem, vmem, vmem, vmem, anywhere, anywhere],
        out_specs=(vmem, vmem),
        scratch_shapes=[
            pltpu.VMEM((BEAMS, 128, 2 * HEAD), BF16),
        ] + [pltpu.VMEM((4, 2, SHARD, 2 * HEAD), BF16)] * 4 + [
            pltpu.VMEM((HOLD * CAP, ROWS, HEAD), BF16),
            pltpu.VMEM((HOLD * CAP, ROWS, HEAD), BF16),
            pltpu.VMEM((HOLD * CAP, ROWS, HEAD), BF16),
            pltpu.VMEM((HOLD * CAP, ROWS, HEAD), BF16),
            pltpu.VMEM((HOLD, 8, 128), F32),
            pltpu.VMEM((HOLD, 8, 128), F32),
            pltpu.VMEM((PLACES, ROWS, HEAD), BF16),
            pltpu.VMEM((PLACES, NEWPAD, 2 * HEAD), BF16),
            pltpu.VMEM((PLACES, ROWS, 2 * HEAD), F32),
            pltpu.VMEM((PLACES, ROWS, 128), F32),
            pltpu.VMEM((BEAMS, 128), F32),
            pltpu.VMEM((8, 128), F32),
            pltpu.VMEM((max(groups, 1), 8, 128), F32),
        ] + [dma((HOLD,))] * 6 + [dma((5,))] * 4 + [dma((8,))] * 2 + [dma((max(groups, 1),))] * 2 + [dma((2,))],
        compiler_params=pltpu.CompilerParams(
            collective_id=0, has_side_effects=True, vmem_limit_bytes=48 * 1024 * 1024),
    )(table, q, kvn, weights, prompt_key_value[0], step_key_value[0])
    return attended.reshape(1, BEAMS, 4, 8 * HEAD), score[0, :BEAMS]


def solution(mesh):
    in_specs = (
        P("grp", "beam", None, "tp"),
        P("grp", "beam", None, "tp"),
        P("grp", None, "beam", "tp"),
        P("grp", "beam", None, "tp"),
        P(),
        P(),
        P(),
        P("beam"),
        P("grp", "tp"),
    )
    out_specs = (P("grp", "beam", None, "tp"), P("beam"))
    return jax.shard_map(on_device, mesh=mesh, in_specs=in_specs, out_specs=out_specs, check_vma=False)
```

time: 500 us -> 139 us (0.28)
  waiting for transfers between devices: 232 us -> 0 us
  Pallas kernels: 0 us -> 126 us
  matrix products: 109 us -> 0 us
  local copies, waits for them, and re-layouts: 52.7 us -> 10.3 us
  blocking collectives: 41.1 us -> 0 us
  other arithmetic: 35.8 us -> 1.96 us
  between operations: 14.3 us -> 0.67 us
  starting transfers between devices: 10.3 us -> 0 us
    all_gather x1 -> x0, waiting for transfers between devices: 232 us -> none  [on_device(): segment = lax.all_gather(prompt_key_value, 'beam', axis=2, tiled=True)]
    pallas_call x0 -> x2, Pallas kernels: none -> 126 us  [the longest x1 124 us: on_device(): pl.pallas_call(functools.partial(main_kernel, groups, lanes_tp), out_shap...]
    dot_general x36 -> x0, matrix products: 109 us -> none  [the longest x16 72.9 us: flash_block(): jnp.einsum('brgjk,kgd->brgjd', weights, value_matrix.astype(jnp.float32),...]
    psum x1 -> x0, blocking collectives: 41.1 us -> none  [on_device(): beam_score = lax.psum(share, ('grp', 'tp'))]
    gather x4 -> x0, local copies, waits for them, and re-layouts: 27.5 us -> none  [the longest x3 18.9 us: on_device(): jnp.take(incoming.reshape((holders * capacity,) + local_pages.shape[1:]),...]
    reduce_sum x11 -> x0, other arithmetic: 22.1 us -> none  [the longest x8 20.5 us: flash_block(): weight_sum = weight_sum * shrink + jnp.sum(weights, axis=-1)]
    while x26 -> x0, local copies, waits for them, and re-layouts: 11.3 us -> none
    all_to_all x1 -> x0, starting transfers between devices: 10.2 us -> none  [on_device(): lax.all_to_all(outgoing, 'beam', split_axis=0, concat_axis=0, tiled=True)]
  transfers between devices with their start and end apart: 2 -> 0, of which waited for: 1 -> 0; matrix products, arithmetic and copies ran while one was open for 31% -> 0% of each run, Pallas kernels for 0% -> 0%
where the time goes in v1:
time: 139 us
  Pallas kernels  126 us (91%)
  local copies, waits for them, and re-layouts  10.3 us (7%)
  other arithmetic  1.96 us (1%)
    pallas_call x1, Pallas kernels, on_device(): pl.pallas_call(functools.partial(main_kernel, groups, lanes_tp), out_shap...  124 us
    unnamed x9, local copies, waits for them, and re-layouts  5.12 us

profile of v1, /device:TPU:1, one launch (start us, length us, event | category | flops | bytes accessed | tf_op | source)
XLA Modules:
  0.0 138.7 jit_solution(17104923132003505237)
XLA Ops:
  0.6 0.0 copy-start
  0.6 0.7 copy-done
  1.3 0.5 broadcast.7
  1.8 1.3 reduce.3
  3.2 0.1 stack.11
  3.3 0.8 stack.12
  4.0 0.8 stack.13
  4.8 0.6 pad_add_fusion.meta_ref
  5.4 1.6 %shard_map.104.tab = s32[88,128]{1,0:T(8,128)} custom-call(s32[3,16,64]{2,1,0:T(8,128)} %pad_add_fusion.meta_ref, s32[1,64]{1,0:T(1,128)} %bitcast.14), custom_call_target="tpu_custom_call" | custom-call | tf_op jit(solution)/shard_map/pallas_call | solution.py:405
  7.0 1.2 reshape.25.q_ref
  8.3 1.0 pad.4.kvn_ref
  9.2 0.0 copy-start.1
  9.2 2.2 %copy-done.1 = bf16[1,64,128,256]{3,2,1,0:T(8,128)(2,1)S(1)} copy-done((bf16[1,64,128,256]{3,2,1,0:T(8,128)(2,1)S(1)}, bf16[1,64,128,256]{3,2,1,0:T(8,128)(2,1)}, u32[]{:S(2)}) %copy-start.1) | copy-done | bytes 4194328
  11.4 0.0 copy-start.2
  11.4 0.9 copy-done.2
  12.4 0.0 copy-start.3
  12.4 0.8 copy-done.3
  13.2 124.1 %shard_map.105 = (bf16[64,32,128]{2,1,0:T(8,128)(2,1)S(1)}, f32[8,128]{1,0:T(8,128)S(1)}) custom-call(s32[88,128]{1,0:T(8,128)S(1)} %copy-done.3, bf16[64,32,128]{2,1,0:T(8,128)(2,1)S(1)} %reshape.25.q_ref, bf16[64,16,256]{2,1,0:T(8,128)(2,1)S(1)} %pad.4.kvn_ref, f32[32,128]{1,0:T(8,128)S(1)} %broadcast_bitcast_fusion.w_ref, ...), custom_call_target="tpu_custom_call" | custom-call | tf_op jit(solution)/shard_map/pallas_call | solution.py:415
  137.3 0.9 reshape.26
  138.2 0.5 slice_bitcast_fusion
  (1 shorter events, 0.0 us)
Async XLA Ops:
  0.6 0.7 copy-start
  9.2 2.2 %copy-start.1 = (bf16[1,64,128,256]{3,2,1,0:T(8,128)(2,1)S(1)}, bf16[1,64,128,256]{3,2,1,0:T(8,128)(2,1)}, u32[]{:S(2)}) copy-start(bf16[1,64,128,256]{3,2,1,0:T(8,128)(2,1)} %param.12) | copy-start | bytes 12582916
  11.4 0.9 copy-start.2
  12.4 0.8 copy-start.3

commit v2 on v1

--- a/solution.py
+++ b/solution.py
@@ -24,61 +24,66 @@
 NEWPAD = 16
 SCALE = math.log2(math.e) / math.sqrt(HEAD)
 LOW = -1e30
-TAB = HOLD + PLACES
+VMEM_LIMIT = 61 * 1024 * 1024
+TAB = 32
+INV, PLACED, PROMPT, ARRIVAL, PLACE = 8, 24, 25, 26, 27
 
 
 def iota(shape, axis):
     return lax.broadcasted_iota(I32, shape, axis)
 
 
-def table_kernel(meta_ref, pid_ref, tab_ref):
+def table_kernel(pdev_ref, slot_ref, length_ref, pid_ref, tab_ref):
     me = lax.axis_index("beam")
-    upper = (iota((BEAMS, BEAMS), 0) < iota((BEAMS, BEAMS), 1)).astype(F32)
-    pdev = meta_ref[0]
-    slot = meta_ref[1].astype(F32)
-    length = meta_ref[2].astype(F32)
-    lane = iota((HOLD, 128), 1)
-    head = jnp.zeros((HOLD, 128), F32)
-
+    z, x = lax.div(me, 2), lax.rem(me, 2)
+    pdev = pdev_ref[...]
+    code = (slot_ref[...] * 256 + length_ref[...]).astype(F32)
+
+    a, b = iota((128, 128), 0), iota((128, 128), 1)
+    upper = ((a < b) & ((a >> 6) == (b >> 6))).astype(F32)
     served = (pdev == me).astype(F32)
     rank = jnp.dot(served, upper, preferred_element_type=F32)
-    mine = meta_ref[0, pl.ds(me, 1), :]
-    ahead = (mine - me + HOLD) & (HOLD - 1)
-    row16 = iota((HOLD, BEAMS), 0)
-    own = (jnp.broadcast_to(ahead, (HOLD, BEAMS)) == row16).astype(F32)
+    lane = iota((8, 128), 1)
+    head = jnp.zeros((8, 128), F32)
+    for k in range(CAP):
+        pick = jnp.where(rank == k, served, 0.0) * code
+        for h in range(2):
+            found = jnp.sum(jnp.where((lane >> 6) == h, pick, 0.0), axis=1, keepdims=True)
+            head = jnp.where(lane == h * CAP + k, found, head)
+    tab_ref[0:8, :] = head.astype(I32)
+
+    upper = upper[:BEAMS, :BEAMS]
+    pair = pdev_ref[pl.ds(z, 1), :]
+    mine = jnp.where(x == 1, pair[:, BEAMS:], pair[:, :BEAMS])
+    ahead = (((mine >> 1) - z) & 7) * 2 + ((mine - x) & 1)
+    offset = iota((HOLD, BEAMS), 0)
+    beam = iota((HOLD, BEAMS), 1).astype(F32)
+    own = (jnp.broadcast_to(ahead, (HOLD, BEAMS)) == offset).astype(F32)
     own_rank = jnp.dot(own, upper, preferred_element_type=F32)
-    beam = iota((HOLD, BEAMS), 1).astype(F32)
+    lane = iota((HOLD, 128), 1)
+    body = jnp.zeros((HOLD, 128), F32)
     for k in range(CAP):
-        pick = jnp.where(rank == k, served, 0.0)
-        head = jnp.where(lane == k, jnp.sum(pick * slot, axis=1, keepdims=True), head)
-        head = jnp.where(lane == CAP + k, jnp.sum(pick * length, axis=1, keepdims=True), head)
-        pick = jnp.where(own_rank == k, own, 0.0)
-        head = jnp.where(lane == 2 * CAP + k, jnp.sum(pick * beam, axis=1, keepdims=True), head)
-    tab_ref[0:HOLD, :] = head.astype(I32)
-
-    arrival = jnp.sum(own * (row16.astype(F32) * CAP + own_rank), axis=0, keepdims=True)
+        found = jnp.sum(jnp.where(own_rank == k, own, 0.0) * beam, axis=1, keepdims=True)
+        body = jnp.where(lane == k, found, body)
+    tab_ref[8:8 + HOLD, :] = body.astype(I32)
+
+    arrival = jnp.sum(own * (offset.astype(F32) * CAP + own_rank), axis=0, keepdims=True)
     first = (pid_ref[...] == 0).astype(F32)
     before = jnp.dot(jnp.broadcast_to(first, (8, BEAMS)), upper, preferred_element_type=F32)[0:1]
     count = jnp.sum(first, axis=1, keepdims=True).astype(I32)
     filled = (count + (TILE - 1)) & (-TILE)
     after = filled.astype(F32) + iota((1, BEAMS), 1).astype(F32) - before
     place = jnp.where(first > 0.5, before, after)
-
-    lane = iota((PLACES, 128), 1)
-    beam = iota((PLACES, BEAMS), 1).astype(F32)
-    here = iota((PLACES, BEAMS), 0).astype(F32)
-    at_place = (jnp.broadcast_to(place, (PLACES, BEAMS)) == here).astype(F32)
-    holder = jnp.sum(at_place * beam, axis=1, keepdims=True)
-    on_diag = (beam == here).astype(F32)
-    arrival_col = jnp.sum(on_diag * arrival, axis=1, keepdims=True)
-    place_col = jnp.sum(on_diag * place, axis=1, keepdims=True)
-    tile_start = iota((PLACES, 128), 0) * TILE
-    which = (tile_start >= filled).astype(F32)
-    body = jnp.where(lane == 0, holder, 0.0)
-    body = jnp.where(lane == 1, which, body)
-    body = jnp.where(lane == 2, arrival_col, body)
-    body = jnp.where(lane == 3, place_col, body)
-    tab_ref[HOLD:TAB, :] = body.astype(I32)
+    diagonal = iota((BEAMS, BEAMS), 0) == iota((BEAMS, BEAMS), 1)
+    column = jnp.sum(jnp.where(diagonal, place, 0.0), axis=1, keepdims=True)
+    there = column == iota((BEAMS, 128), 1).astype(F32)
+    holder = jnp.sum(jnp.where(there, iota((BEAMS, 128), 0).astype(F32), 0.0), axis=0, keepdims=True)
+    which = (iota((1, 128), 1) * TILE >= filled).astype(F32)
+    rest = jnp.zeros((1, 128 - BEAMS), F32)
+    tail = jnp.concatenate([
+        holder, which, jnp.concatenate([arrival, rest], axis=1), jnp.concatenate([place, rest], axis=1),
+        jnp.zeros((4, 128), F32)], axis=0)
+    tab_ref[24:32, :] = tail.astype(I32)
 
 
 OWN, XOWN, ANTI, XANTI = 0, 1, 14, 15
@@ -97,9 +102,9 @@
 
 
 def main_kernel(
-    groups, lanes_tp, tab, q_ref, kvn_ref, w_ref, prompt_hbm, pages_hbm,
+    groups, lanes_tp, tab_any, q_ref, kvn_ref, w_ref, prompt_hbm, pages_hbm,
     out_ref, score_ref,
-    pages, kv0, kv1, kv2, kv3, send, recv, ret_out, ret_in, stat_out, stat_in,
+    tab, pages, kv0, kv1, kv2, kv3, send, recv, ret_out, ret_in, stat_out, stat_in,
     qt, kvt, acc, high, part, share, shares,
     q_ss, q_rs, r_ss, r_rs, s_ss, s_rs, f_ss, f_rs, b_ss, b_rs, x_ss, x_rs, c_ss, c_rs, l_sem,
 ):
@@ -107,9 +112,22 @@
     grp = lax.axis_index("grp")
     tp = lax.axis_index("tp")
     group = grp * lanes_tp + tp
-    up = lax.rem(me + 2, HOLD)
-    down = lax.rem(me + HOLD - 2, HOLD)
-    side = me + 1 - 2 * lax.rem(me, 2)
+    z, x = lax.div(me, 2), lax.rem(me, 2)
+
+    def at(dz, dx):
+        return lax.rem(z + dz + 8, 8) * 2 + lax.rem(x + dx, 2)
+
+    def target(o):
+        return at(lax.div(o, 2), lax.rem(o, 2))
+
+    def origin(o):
+        return at(-lax.div(o, 2), lax.rem(o, 2))
+
+    def near(i):
+        g, r = lax.div(i - 1, 4), lax.rem(i - 1, 4)
+        return (g + 1 + lax.div(r, 2) * (6 - 2 * g)) * 2 + lax.rem(r, 2)
+
+    up, down, side = at(1, 0), at(-1, 0), at(0, 1)
 
     held = (kv0, kv1, kv2, kv3)
 
@@ -118,6 +136,8 @@
 
     load_prompt = pltpu.make_async_copy(prompt_hbm, shard_at(OWN), l_sem.at[0])
     load_pages = pltpu.make_async_copy(pages_hbm, pages, l_sem.at[1])
+    load_table = pltpu.make_async_copy(tab_any, tab, l_sem.at[2])
+    load_table.start()
     load_prompt.start()
     load_pages.start()
 
@@ -143,24 +163,29 @@
     def span(o):
         return pl.ds(o * CAP, CAP)
 
+    load_table.wait()
+
     def pack(o, into):
         for k in range(CAP):
-            into[o * CAP + k] = q_ref[tab[o, 2 * CAP + k]]
+            into[o * CAP + k] = q_ref[tab[INV + o, k]]
+
+    def pack_for(o, _):
+        pack(o, send)
+        return 0
 
     pack(0, recv)
+    lax.fori_loop(1, HOLD, pack_for, 0)
+    load_prompt.wait()
     pl.semaphore_wait(barrier, HOLD - 1 + groups - 1)
 
     def query_copy(o):
         return pltpu.make_async_remote_copy(
             src_ref=send.at[span(o)], dst_ref=recv.at[span(o)], send_sem=q_ss.at[o], recv_sem=q_rs.at[o],
-            device_id={"beam": lax.rem(me + o, HOLD)}, device_id_type=MESH)
-
-    def send_query(o, _):
-        pack(o, send)
-        query_copy(o).start()
-        return 0
-
-    lax.fori_loop(1, HOLD, send_query, 0)
+            device_id={"beam": target(o)}, device_id_type=MESH)
+
+    def send_near(i, _):
+        query_copy(near(i)).start()
+        return 0
 
     def shard_copy(src, dst, to, ss, rs, half=None):
         a, b = shard_at(src), shard_at(dst)
@@ -190,10 +215,11 @@
         src, dst = x_plan[i]
         return shard_copy(src, dst, side, x_ss.at[i], x_rs.at[i])
 
-    load_prompt.wait()
     fwd_copy(1).start()
     bwd_copy(1).start()
     x_copy(0).start()
+    query_copy(1).start()
+    lax.fori_loop(1, 5, send_near, 0)
 
     def ring_step(s):
         fwd_copy(s).wait_recv()
@@ -209,7 +235,7 @@
 
     def fill_tile(t, _):
         for i in range(TILE):
-            b = tab[HOLD + t * TILE + i, 0]
+            b = tab[PLACED, t * TILE + i]
             qt[t * TILE + i] = q_ref[b]
             kvt[t * TILE + i] = kvn_ref[b]
         return 0
@@ -223,18 +249,20 @@
     column = iota((ROWS, 128), 1)
 
     def step_part(o, into_out, into_stat):
-        c = lax.rem(me - o + HOLD, HOLD)
+        c = origin(o)
+        row, lane = lax.div(c, 2), lax.rem(c, 2) * CAP
         blocks = []
         values = []
         for j in range(CAP // 2):
-            k0, k1 = 2 * j, 2 * j + 1
-            page0, page1 = pages[tab[c, k0]], pages[tab[c, k1]]
+            k0 = 2 * j
+            code0, code1 = tab[row, lane + k0], tab[row, lane + k0 + 1]
+            page0, page1 = pages[code0 >> 8], pages[code1 >> 8]
             keys = jnp.concatenate([page0[:, :HEAD], page1[:, :HEAD]], axis=0)
             values.append(with_ones(jnp.concatenate([page0[:, HEAD:], page1[:, HEAD:]], axis=0)))
             queries = recv[pl.ds(o * CAP + k0, 2)].reshape(2 * ROWS, HEAD)
             s = dot_nt(queries, keys)
-            blocks.append(jnp.where(column < tab[c, CAP + k0], s[:ROWS, :128] * SCALE, LOW))
-            blocks.append(jnp.where(column < tab[c, CAP + k1], s[ROWS:, 128:] * SCALE, LOW))
+            blocks.append(jnp.where(column < (code0 & 255), s[:ROWS, :128] * SCALE, LOW))
+            blocks.append(jnp.where(column < (code1 & 255), s[ROWS:, 128:] * SCALE, LOW))
         s = jnp.concatenate(blocks, axis=0)
         top = jnp.max(s, axis=1, keepdims=True)
         p = jnp.exp2(s - top).astype(BF16)
@@ -253,7 +281,7 @@
         into_stat[o] = jnp.concatenate([flat, jnp.zeros((6, 128), F32)], axis=0)
 
     def back_copy(o):
-        to = {"beam": lax.rem(me - o + HOLD, HOLD)}
+        to = {"beam": origin(o)}
         return (
             pltpu.make_async_remote_copy(
                 src_ref=ret_out.at[span(o)], dst_ref=ret_in.at[span(o)], send_sem=r_ss.at[o],
@@ -263,15 +291,13 @@
                 recv_sem=s_rs.at[o], device_id=to, device_id_type=MESH),
         )
 
-    def serve(o, _):
+    def serve(i, _):
+        o = near(i)
         query_copy(o).wait_recv()
         step_part(o, ret_out, stat_out)
         for copy in back_copy(o):
             copy.start()
         return 0
-
-    load_pages.wait()
-    step_part(0, ret_in, stat_in)
 
     def new_part(t, _):
         q = qt[pl.ds(t * TILE, TILE)].reshape(TROWS, HEAD)
@@ -285,38 +311,52 @@
         high[pl.ds(t * TILE, TILE)] = jnp.broadcast_to(top, (TROWS, 128)).reshape(TILE, ROWS, 128)
         return 0
 
-    lax.fori_loop(0, TILES, new_part, 0)
-
-    lax.fori_loop(1, 5, serve, 0)
-    ring_step(1)
-    lax.fori_loop(5, 9, serve, 0)
-    ring_step(2)
-    lax.fori_loop(9, 13, serve, 0)
-    ring_step(3)
-    lax.fori_loop(13, 16, serve, 0)
-
     def prompt_part(number):
-        def one(t, _):
-            own = tab[HOLD + t, 1]
+        def one(t):
+            own = tab[PROMPT, t]
             q = qt[pl.ds(t * TILE, TILE)].reshape(TROWS, HEAD)
             kv = held[number][:, own].reshape(4 * SHARD, 2 * HEAD)
-            s = dot_nt(q, kv[:, :HEAD]) * SCALE
+            s = dot_nt(q, kv[:, :HEAD])
+            cols = [s[:, i * 128:(i + 1) * 128] for i in range(4 * SHARD // 128)]
+            top = functools.reduce(jnp.maximum, cols)
             old = high[pl.ds(t * TILE, TILE)].reshape(TROWS, 128)
-            top = jnp.maximum(old, jnp.max(s, axis=1, keepdims=True))
-            p = jnp.exp2(s - top[:, :1]).astype(BF16)
+            top = jnp.maximum(old, jnp.max(top, axis=1, keepdims=True) * SCALE)
+            p = jnp.concatenate([jnp.exp2(col * SCALE - top).astype(BF16) for col in cols], axis=1)
             fade = jnp.exp2(old - top)
             add = dot_nn(p, with_ones(kv[:, HEAD:]))
             was = acc[pl.ds(t * TILE, TILE)].reshape(TROWS, 2 * HEAD)
             new = was * jnp.concatenate([fade, fade], axis=1) + add
             acc[pl.ds(t * TILE, TILE)] = new.reshape(TILE, ROWS, 2 * HEAD)
             high[pl.ds(t * TILE, TILE)] = top.reshape(TILE, ROWS, 128)
+
+        def some(i, _):
+            for u in range(3):
+                one(i * 3 + u)
             return 0
 
-        lax.fori_loop(0, TILES, one, 0)
-
+        lax.fori_loop(0, TILES // 3, some, 0)
+
+    def query_first(_):
+        query_copy(1).wait_recv()
+        step_part(1, ret_out, stat_out)
+        for copy in back_copy(1):
+            copy.start()
+
+    load_pages.wait()
+    step_part(0, ret_in, stat_in)
+    lax.fori_loop(0, TILES, new_part, 0)
+    ring_step(1)
+    lax.fori_loop(5, 9, send_near, 0)
+    ring_step(2)
+    lax.fori_loop(9, 15, send_near, 0)
+    query_first(0)
+    lax.fori_loop(1, 5, serve, 0)
+    ring_step(3)
     x_copy(0).wait_recv()
     prompt_part(0)
+    lax.fori_loop(5, 9, serve, 0)
     ring_step(4)
+    lax.fori_loop(9, 15, serve, 0)
     for i in (1, 2):
         x_copy(i).wait_recv()
     prompt_part(1)
@@ -336,11 +376,13 @@
 
     lane_of = iota((ROWS, 128), 1) - iota((ROWS, 128), 0)
 
+    weights = jnp.concatenate([w_ref[...]] * 4, axis=0)
+
     def finish(i, _):
         for u in range(4):
             b = i * 4 + u
-            a = tab[HOLD + b, 2]
-            place = tab[HOLD + b, 3]
+            a = tab[ARRIVAL, b]
+            place = tab[PLACE, b]
             line = stat_in[a >> 3, pl.ds((a >> 2) & 1, 1), :]
             level = jnp.sum(jnp.where(lane_of == (a & 3) * ROWS, line, 0.0), axis=1, keepdims=True)
             old = high[place]
@@ -350,7 +392,7 @@
             whole = sums[:, :HEAD] * mine + ret_in[a].astype(F32) * theirs
             result = (whole / (sums[:, HEAD:] * mine + theirs)).astype(BF16)
             out_ref[b] = result
-            part[pl.ds(b, 1), :] = jnp.sum(result.astype(F32) * w_ref[...], axis=0, keepdims=True)
+            part[pl.ds(b, 1), :] = jnp.sum(result.astype(F32) * weights, axis=0, keepdims=True)
         return 0
 
     lax.fori_loop(0, BEAMS // 4, finish, 0)
@@ -398,19 +440,19 @@
 def on_device(queries, new_kv, prompt_key_value, step_key_value, parent_dev, parent_slot, cache_len, prompt_ids, score_weights):
     lanes_tp = lax.axis_size("tp")
     groups = lax.axis_size("grp") * lanes_tp
-    meta = jnp.stack([parent_dev[:, 0], parent_slot, cache_len]).reshape(3, HOLD, BEAMS)
     vmem = pl.BlockSpec(memory_space=pltpu.VMEM)
-    smem = pl.BlockSpec(memory_space=pltpu.SMEM)
+    hbm = pl.BlockSpec(memory_space=pltpu.HBM)
     anywhere = pl.BlockSpec(memory_space=pl.ANY)
     table = pl.pallas_call(
         table_kernel,
         out_shape=jax.ShapeDtypeStruct((TAB, 128), I32),
-        in_specs=[vmem, vmem],
+        in_specs=[vmem] * 4,
         out_specs=vmem,
-    )(meta, prompt_ids.reshape(1, BEAMS))
+        compiler_params=pltpu.CompilerParams(vmem_limit_bytes=VMEM_LIMIT),
+    )(parent_dev.reshape(8, 128), parent_slot.reshape(8, 128), cache_len.reshape(8, 128), prompt_ids.reshape(1, BEAMS))
     q = queries.reshape(BEAMS, ROWS, HEAD)
     kvn = jnp.pad(new_kv[0], ((0, 0), (0, NEWPAD - new_kv.shape[2]), (0, 0)))
-    weights = jnp.tile(score_weights.reshape(8, HEAD), (4, 1))
+    weights = score_weights.reshape(8, HEAD)
     dma = pltpu.SemaphoreType.DMA
     attended, score = pl.pallas_call(
         functools.partial(main_kernel, groups, lanes_tp),
@@ -418,9 +460,10 @@
             jax.ShapeDtypeStruct((BEAMS, ROWS, HEAD), BF16),
             jax.ShapeDtypeStruct((8, 128), F32),
         ),
-        in_specs=[smem, vmem, vmem, vmem, anywhere, anywhere],
+        in_specs=[anywhere, vmem, vmem, vmem, hbm, hbm],
         out_specs=(vmem, vmem),
         scratch_shapes=[
+            pltpu.SMEM((TAB, 128), I32),
             pltpu.VMEM((BEAMS, 128, 2 * HEAD), BF16),
         ] + [pltpu.VMEM((4, 2, SHARD, 2 * HEAD), BF16)] * 4 + [
             pltpu.VMEM((HOLD * CAP, ROWS, HEAD), BF16),
@@ -436,9 +479,9 @@
             pltpu.VMEM((BEAMS, 128), F32),
             pltpu.VMEM((8, 128), F32),
             pltpu.VMEM((max(groups, 1), 8, 128), F32),
-        ] + [dma((HOLD,))] * 6 + [dma((5,))] * 4 + [dma((8,))] * 2 + [dma((max(groups, 1),))] * 2 + [dma((2,))],
+        ] + [dma((HOLD,))] * 6 + [dma((5,))] * 4 + [dma((8,))] * 2 + [dma((max(groups, 1),))] * 2 + [dma((3,))],
         compiler_params=pltpu.CompilerParams(
-            collective_id=0, has_side_effects=True, vmem_limit_bytes=48 * 1024 * 1024),
+            collective_id=0, has_side_effects=True, vmem_limit_bytes=VMEM_LIMIT),
     )(table, q, kvn, weights, prompt_key_value[0], step_key_value[0])
     return attended.reshape(1, BEAMS, 4, 8 * HEAD), score[0, :BEAMS]
 

time: 139 us -> 105 us (0.76)
  Pallas kernels: 126 us -> 97.5 us
  local copies, waits for them, and re-layouts: 10.3 us -> 6.91 us
  other arithmetic: 1.96 us -> 0 us
    pallas_call x1, Pallas kernels: 124 us -> 95.8 us  [on_device(): pl.pallas_call(functools.partial(main_kernel, groups, lanes_tp), out_shap...]
    unnamed x9 -> x0, local copies, waits for them, and re-layouts: 5.12 us -> none
    another operation x4 -> x0, local copies, waits for them, and re-layouts: 1.58 us -> none  [the longest x3 1.58 us: on_device(): jnp.stack([parent_dev[:, 0], parent_slot, cache_len])]
where the time goes in v2:
time: 105 us
  Pallas kernels  97.5 us (93%)
  local copies, waits for them, and re-layouts  6.91 us (7%)
    pallas_call x1, Pallas kernels, on_device(): pl.pallas_call(functools.partial(main_kernel, groups, lanes_tp), out_shap...  95.8 us

profile of v2, /device:TPU:1, one launch (start us, length us, event | category | flops | bytes accessed | tf_op | source)
XLA Modules:
  0.0 105.1 jit_solution(16334344449123890731)
XLA Ops:
  0.6 1.7 %shard_map.104.tab_any = s32[32,128]{1,0:T(8,128)} custom-call(s32[8,128]{1,0:T(8,128)} %bitcast.14, s32[8,128]{1,0:T(8,128)} %bitcast.15, s32[8,128]{1,0:T(8,128)} %bitcast.16, s32[1,64]{1,0:T(1,128)} %bitcast.17), custom_call_target="tpu_custom_call" | custom-call | tf_op jit(solution)/shard_map/pallas_call | solution.py:446
  2.4 2.0 %reshape.29.q_ref = bf16[64,32,128]{2,1,0:T(8,128)(2,1)} reshape(bf16[1,64,4,1024]{3,2,1,0:T(4,128)(2,1)} %param.9) | data formatting | bytes 1048576 | tf_op jit(solution)/shard_map/reshape | solution.py:453
  4.4 1.7 %pad.4.kvn_ref = bf16[64,16,256]{2,1,0:T(8,128)(2,1)} pad(bf16[64,4,256]{2,1,0:T(4,128)(2,1)} %bitcast.12, bf16[]{:T(256)} %constant.2.clone.1), padding=0_0x0_12x0_0 | pad | bytes 655362 | tf_op jit(solution)/shard_map/jit(_pad)/pad | solution.py:454
  6.1 95.8 %shard_map.105 = (bf16[64,32,128]{2,1,0:T(8,128)(2,1)}, f32[8,128]{1,0:T(8,128)}) custom-call(s32[32,128]{1,0:T(8,128)} %shard_map.104.tab_any, bf16[64,32,128]{2,1,0:T(8,128)(2,1)} %reshape.29.q_ref, bf16[64,16,256]{2,1,0:T(8,128)(2,1)} %pad.4.kvn_ref, f32[8,128]{1,0:T(8,128)} %bitcast.13, bf16[2,256,256]{2,1,0:T(8,128)(2,1)} %bitcast.11, ...), custom_call_target="tpu_custom_call" | custom-call | tf_op jit(solution)/shard_map/pallas_call | solution.py:457
  101.9 2.0 %reshape.31 = bf16[1,64,4,1024]{3,2,1,0:T(4,128)(2,1)} reshape(bf16[64,32,128]{2,1,0:T(8,128)(2,1)} %get-tuple-element.4) | data formatting | bytes 1048576 | tf_op jit(solution)/shard_map/reshape | solution.py:486
  103.9 1.2 %slice_bitcast_fusion = f32[64]{0:T(128)} fusion(f32[8,128]{1,0:T(8,128)} %get-tuple-element.5), kind=kLoop, calls=%fused_computation | loop fusion | bytes 512 | tf_op jit(solution)/shard_map/squeeze | solution.py:486

commit v3 on v2

--- a/solution.py
+++ b/solution.py
@@ -21,7 +21,7 @@
 PLACES = TILES * TILE
 TROWS = TILE * ROWS
 SHARD = 256
-NEWPAD = 16
+NEW = 8
 SCALE = math.log2(math.e) / math.sqrt(HEAD)
 LOW = -1e30
 VMEM_LIMIT = 61 * 1024 * 1024
@@ -33,7 +33,7 @@
     return lax.broadcasted_iota(I32, shape, axis)
 
 
-def table_kernel(pdev_ref, slot_ref, length_ref, pid_ref, tab_ref):
+def make_table(pdev_ref, slot_ref, length_ref, pid_ref, tab_ref):
     me = lax.axis_index("beam")
     z, x = lax.div(me, 2), lax.rem(me, 2)
     pdev = pdev_ref[...]
@@ -67,7 +67,7 @@
         body = jnp.where(lane == k, found, body)
     tab_ref[8:8 + HOLD, :] = body.astype(I32)
 
-    arrival = jnp.sum(own * (offset.astype(F32) * CAP + own_rank), axis=0, keepdims=True)
+    arrival = jnp.sum(own * (offset.astype(F32) * CAP + jnp.minimum(own_rank, CAP - 1)), axis=0, keepdims=True)
     first = (pid_ref[...] == 0).astype(F32)
     before = jnp.dot(jnp.broadcast_to(first, (8, BEAMS)), upper, preferred_element_type=F32)[0:1]
     count = jnp.sum(first, axis=1, keepdims=True).astype(I32)
@@ -102,9 +102,9 @@
 
 
 def main_kernel(
-    groups, lanes_tp, tab_any, q_ref, kvn_ref, w_ref, prompt_hbm, pages_hbm,
+    groups, lanes_tp, pdev_ref, slot_ref, length_ref, pid_ref, w_ref, q_hbm, kvn_hbm, prompt_hbm, pages_hbm,
     out_ref, score_ref,
-    tab, pages, kv0, kv1, kv2, kv3, send, recv, ret_out, ret_in, stat_out, stat_in,
+    table, tab, q_ref, kvn_ref, pages, kv0, kv1, kv2, kv3, kv4, send, recv, ret_out, ret_in, stat_out, stat_in,
     qt, kvt, acc, high, part, share, shares,
     q_ss, q_rs, r_ss, r_rs, s_ss, s_rs, f_ss, f_rs, b_ss, b_rs, x_ss, x_rs, c_ss, c_rs, l_sem,
 ):
@@ -129,17 +129,19 @@
 
     up, down, side = at(1, 0), at(-1, 0), at(0, 1)
 
-    held = (kv0, kv1, kv2, kv3)
+    held = (kv0, kv1, kv2, kv3, kv4)
 
     def shard_at(slot):
+        if slot == XANTI:
+            return kv4.at[0]
         return held[slot // 4].at[slot % 4]
 
     load_prompt = pltpu.make_async_copy(prompt_hbm, shard_at(OWN), l_sem.at[0])
     load_pages = pltpu.make_async_copy(pages_hbm, pages, l_sem.at[1])
-    load_table = pltpu.make_async_copy(tab_any, tab, l_sem.at[2])
-    load_table.start()
-    load_prompt.start()
-    load_pages.start()
+    load_queries = pltpu.make_async_copy(q_hbm, q_ref, l_sem.at[3])
+    load_new = pltpu.make_async_copy(kvn_hbm, kvn_ref, l_sem.at[4])
+    for load in (load_prompt, load_queries, load_new, load_pages):
+        load.start()
 
     barrier = pltpu.get_barrier_semaphore()
 
@@ -159,33 +161,6 @@
             return 0
 
         lax.fori_loop(1, groups, greet_group, 0)
-
-    def span(o):
-        return pl.ds(o * CAP, CAP)
-
-    load_table.wait()
-
-    def pack(o, into):
-        for k in range(CAP):
-            into[o * CAP + k] = q_ref[tab[INV + o, k]]
-
-    def pack_for(o, _):
-        pack(o, send)
-        return 0
-
-    pack(0, recv)
-    lax.fori_loop(1, HOLD, pack_for, 0)
-    load_prompt.wait()
-    pl.semaphore_wait(barrier, HOLD - 1 + groups - 1)
-
-    def query_copy(o):
-        return pltpu.make_async_remote_copy(
-            src_ref=send.at[span(o)], dst_ref=recv.at[span(o)], send_sem=q_ss.at[o], recv_sem=q_rs.at[o],
-            device_id={"beam": target(o)}, device_id_type=MESH)
-
-    def send_near(i, _):
-        query_copy(near(i)).start()
-        return 0
 
     def shard_copy(src, dst, to, ss, rs, half=None):
         a, b = shard_at(src), shard_at(dst)
@@ -215,11 +190,42 @@
         src, dst = x_plan[i]
         return shard_copy(src, dst, side, x_ss.at[i], x_rs.at[i])
 
+    load_prompt.wait()
+    pl.semaphore_wait(barrier, HOLD - 1 + groups - 1)
     fwd_copy(1).start()
     bwd_copy(1).start()
     x_copy(0).start()
+
+    make_table(pdev_ref, slot_ref, length_ref, pid_ref, table)
+    load_table = pltpu.make_async_copy(table, tab, l_sem.at[2])
+    load_table.start()
+    load_table.wait()
+
+    load_queries.wait()
+    def span(o):
+        return pl.ds(o * CAP, CAP)
+
+    def pack(o, into):
+        for k in range(CAP):
+            into[o * CAP + k] = q_ref[tab[INV + o, k] & (BEAMS - 1)]
+
+
+    def query_copy(o):
+        return pltpu.make_async_remote_copy(
+            src_ref=send.at[span(o)], dst_ref=recv.at[span(o)], send_sem=q_ss.at[o], recv_sem=q_rs.at[o],
+            device_id={"beam": target(o)}, device_id_type=MESH)
+
+    def send_near(i, _):
+        o = near(i)
+        pack(o, send)
+        query_copy(o).start()
+        return 0
+
+    pack(1, send)
     query_copy(1).start()
     lax.fori_loop(1, 5, send_near, 0)
+    pack(0, recv)
+    load_new.wait()
 
     def ring_step(s):
         fwd_copy(s).wait_recv()
@@ -235,9 +241,9 @@
 
     def fill_tile(t, _):
         for i in range(TILE):
-            b = tab[PLACED, t * TILE + i]
+            b = tab[PLACED, t * TILE + i] & (BEAMS - 1)
             qt[t * TILE + i] = q_ref[b]
-            kvt[t * TILE + i] = kvn_ref[b]
+            kvt[t * TILE + i] = kvn_ref[b].astype(F32)
         return 0
 
     lax.fori_loop(0, TILES, fill_tile, 0)
@@ -256,7 +262,7 @@
         for j in range(CAP // 2):
             k0 = 2 * j
             code0, code1 = tab[row, lane + k0], tab[row, lane + k0 + 1]
-            page0, page1 = pages[code0 >> 8], pages[code1 >> 8]
+            page0, page1 = pages[(code0 >> 8) & (BEAMS - 1)], pages[(code1 >> 8) & (BEAMS - 1)]
             keys = jnp.concatenate([page0[:, :HEAD], page1[:, :HEAD]], axis=0)
             values.append(with_ones(jnp.concatenate([page0[:, HEAD:], page1[:, HEAD:]], axis=0)))
             queries = recv[pl.ds(o * CAP + k0, 2)].reshape(2 * ROWS, HEAD)
@@ -278,7 +284,7 @@
         into_out[span(o)] = (sums[:, :HEAD] / total).astype(BF16).reshape(CAP, ROWS, HEAD)
         level = top + jnp.log2(total)
         flat = jnp.sum(jnp.where(diag, level, 0.0).reshape(2, 128, 128), axis=1)
-        into_stat[o] = jnp.concatenate([flat, jnp.zeros((6, 128), F32)], axis=0)
+        into_stat[o] = flat
 
     def back_copy(o):
         to = {"beam": origin(o)}
@@ -301,23 +307,26 @@
 
     def new_part(t, _):
         q = qt[pl.ds(t * TILE, TILE)].reshape(TROWS, HEAD)
-        kv = kvt[pl.ds(t * TILE, TILE)].reshape(TILE * NEWPAD, 2 * HEAD)
-        row, col = iota((TROWS, TILE * NEWPAD), 0), iota((TROWS, TILE * NEWPAD), 1)
-        seen = ((row >> 5) == (col >> 4)) & ((col & 15) <= ((row >> 3) & 3))
-        s = jnp.where(seen, dot_nt(q, kv[:, :HEAD]) * SCALE, LOW)
+        kv = kvt[pl.ds(t * TILE, TILE)].reshape(TILE * NEW, HEAD)
+        kv = jnp.concatenate([kv, jnp.zeros(kv.shape, F32)], axis=0).astype(BF16)
+        row, col = iota((TROWS, 128), 0), iota((TROWS, 128), 1)
+        seen = ((row >> 5) == (col >> 3)) & ((col & 7) <= (row & 3))
+        s = jnp.where(seen, dot_nt(q, kv) * SCALE, LOW)
         top = jnp.max(s, axis=1, keepdims=True)
-        p = jnp.exp2(s - top).astype(BF16)
-        acc[pl.ds(t * TILE, TILE)] = dot_nn(p, with_ones(kv[:, HEAD:])).reshape(TILE, ROWS, 2 * HEAD)
+        p = pltpu.roll(jnp.exp2(s - top), 4, 1).astype(BF16)
+        acc[pl.ds(t * TILE, TILE)] = dot_nn(p, with_ones(kv)).reshape(TILE, ROWS, 2 * HEAD)
         high[pl.ds(t * TILE, TILE)] = jnp.broadcast_to(top, (TROWS, 128)).reshape(TILE, ROWS, 128)
         return 0
 
     def prompt_part(number):
+        keys = held[number].shape[0] * SHARD
+
         def one(t):
-            own = tab[PROMPT, t]
+            own = tab[PROMPT, t] & 1
             q = qt[pl.ds(t * TILE, TILE)].reshape(TROWS, HEAD)
-            kv = held[number][:, own].reshape(4 * SHARD, 2 * HEAD)
+            kv = held[number][:, own].reshape(keys, 2 * HEAD)
             s = dot_nt(q, kv[:, :HEAD])
-            cols = [s[:, i * 128:(i + 1) * 128] for i in range(4 * SHARD // 128)]
+            cols = [s[:, i * 128:(i + 1) * 128] for i in range(keys // 128)]
             top = functools.reduce(jnp.maximum, cols)
             old = high[pl.ds(t * TILE, TILE)].reshape(TROWS, 128)
             top = jnp.maximum(old, jnp.max(top, axis=1, keepdims=True) * SCALE)
@@ -352,20 +361,22 @@
     query_first(0)
     lax.fori_loop(1, 5, serve, 0)
     ring_step(3)
-    x_copy(0).wait_recv()
-    prompt_part(0)
     lax.fori_loop(5, 9, serve, 0)
     ring_step(4)
     lax.fori_loop(9, 15, serve, 0)
+    x_copy(0).wait_recv()
+    prompt_part(0)
     for i in (1, 2):
         x_copy(i).wait_recv()
     prompt_part(1)
     for i in (3, 4):
         x_copy(i).wait_recv()
     prompt_part(2)
-    for i in (5, 6, 7):
+    for i in (5, 6):
         x_copy(i).wait_recv()
     prompt_part(3)
+    x_copy(7).wait_recv()
+    prompt_part(4)
 
     def await_back(o, _):
         for copy in back_copy(o):
@@ -376,13 +387,16 @@
 
     lane_of = iota((ROWS, 128), 1) - iota((ROWS, 128), 0)
 
-    weights = jnp.concatenate([w_ref[...]] * 4, axis=0)
+    head_of = iota((ROWS, 128), 0) >> 2
+    weights = jnp.zeros((ROWS, 128), F32)
+    for j in range(8):
+        weights = jnp.where(head_of == j, w_ref[j:j + 1, :], weights)
 
     def finish(i, _):
         for u in range(4):
             b = i * 4 + u
-            a = tab[ARRIVAL, b]
-            place = tab[PLACE, b]
+            a = tab[ARRIVAL, b] & (HOLD * CAP - 1)
+            place = jnp.clip(tab[PLACE, b], 0, PLACES - 1)
             line = stat_in[a >> 3, pl.ds((a >> 2) & 1, 1), :]
             level = jnp.sum(jnp.where(lane_of == (a & 3) * ROWS, line, 0.0), axis=1, keepdims=True)
             old = high[place]
@@ -442,16 +456,8 @@
     groups = lax.axis_size("grp") * lanes_tp
     vmem = pl.BlockSpec(memory_space=pltpu.VMEM)
     hbm = pl.BlockSpec(memory_space=pltpu.HBM)
-    anywhere = pl.BlockSpec(memory_space=pl.ANY)
-    table = pl.pallas_call(
-        table_kernel,
-        out_shape=jax.ShapeDtypeStruct((TAB, 128), I32),
-        in_specs=[vmem] * 4,
-        out_specs=vmem,
-        compiler_params=pltpu.CompilerParams(vmem_limit_bytes=VMEM_LIMIT),
-    )(parent_dev.reshape(8, 128), parent_slot.reshape(8, 128), cache_len.reshape(8, 128), prompt_ids.reshape(1, BEAMS))
-    q = queries.reshape(BEAMS, ROWS, HEAD)
-    kvn = jnp.pad(new_kv[0], ((0, 0), (0, NEWPAD - new_kv.shape[2]), (0, 0)))
+    q = queries.reshape(BEAMS, 4, 8, HEAD).transpose(0, 2, 1, 3).reshape(BEAMS, ROWS, HEAD)
+    kvn = new_kv.reshape(BEAMS, 4, 2, HEAD).transpose(0, 2, 1, 3).reshape(BEAMS, NEW, HEAD)
     weights = score_weights.reshape(8, HEAD)
     dma = pltpu.SemaphoreType.DMA
     attended, score = pl.pallas_call(
@@ -460,29 +466,34 @@
             jax.ShapeDtypeStruct((BEAMS, ROWS, HEAD), BF16),
             jax.ShapeDtypeStruct((8, 128), F32),
         ),
-        in_specs=[anywhere, vmem, vmem, vmem, hbm, hbm],
+        in_specs=[vmem] * 5 + [hbm] * 4,
         out_specs=(vmem, vmem),
         scratch_shapes=[
+            pltpu.VMEM((TAB, 128), I32),
             pltpu.SMEM((TAB, 128), I32),
+            pltpu.VMEM((BEAMS, ROWS, HEAD), BF16),
+            pltpu.VMEM((BEAMS, NEW, HEAD), BF16),
             pltpu.VMEM((BEAMS, 128, 2 * HEAD), BF16),
-        ] + [pltpu.VMEM((4, 2, SHARD, 2 * HEAD), BF16)] * 4 + [
+        ] + [pltpu.VMEM((n, 2, SHARD, 2 * HEAD), BF16) for n in (4, 4, 4, 3, 1)] + [
             pltpu.VMEM((HOLD * CAP, ROWS, HEAD), BF16),
             pltpu.VMEM((HOLD * CAP, ROWS, HEAD), BF16),
             pltpu.VMEM((HOLD * CAP, ROWS, HEAD), BF16),
             pltpu.VMEM((HOLD * CAP, ROWS, HEAD), BF16),
-            pltpu.VMEM((HOLD, 8, 128), F32),
-            pltpu.VMEM((HOLD, 8, 128), F32),
+            pltpu.VMEM((HOLD, 2, 128), F32),
+            pltpu.VMEM((HOLD, 2, 128), F32),
             pltpu.VMEM((PLACES, ROWS, HEAD), BF16),
-            pltpu.VMEM((PLACES, NEWPAD, 2 * HEAD), BF16),
+            pltpu.VMEM((PLACES, NEW, HEAD), F32),
             pltpu.VMEM((PLACES, ROWS, 2 * HEAD), F32),
             pltpu.VMEM((PLACES, ROWS, 128), F32),
             pltpu.VMEM((BEAMS, 128), F32),
             pltpu.VMEM((8, 128), F32),
             pltpu.VMEM((max(groups, 1), 8, 128), F32),
-        ] + [dma((HOLD,))] * 6 + [dma((5,))] * 4 + [dma((8,))] * 2 + [dma((max(groups, 1),))] * 2 + [dma((3,))],
+        ] + [dma((HOLD,))] * 6 + [dma((5,))] * 4 + [dma((8,))] * 2 + [dma((max(groups, 1),))] * 2 + [dma((5,))],
         compiler_params=pltpu.CompilerParams(
             collective_id=0, has_side_effects=True, vmem_limit_bytes=VMEM_LIMIT),
-    )(table, q, kvn, weights, prompt_key_value[0], step_key_value[0])
+    )(parent_dev.reshape(8, 128), parent_slot.reshape(8, 128), cache_len.reshape(8, 128), prompt_ids.reshape(1, BEAMS),
+      weights, q, kvn, prompt_key_value[0], step_key_value[0])
+    attended = attended.reshape(BEAMS, 8, 4, HEAD).transpose(0, 2, 1, 3)
     return attended.reshape(1, BEAMS, 4, 8 * HEAD), score[0, :BEAMS]
 
 

time: 105 us -> 96.4 us (0.918)
  Pallas kernels: 97.5 us -> 92.3 us
  local copies, waits for them, and re-layouts: 6.91 us -> 3.2 us
    reshape x2 -> x0, local copies, waits for them, and re-layouts: 3.99 us -> none  [the longest x1 2.03 us: on_device(): q = queries.reshape(BEAMS, ROWS, HEAD)]
    pallas_call x1, Pallas kernels: 95.8 us -> 92.3 us  [on_device(): pl.pallas_call(functools.partial(main_kernel, groups, lanes_tp), out_shap...]
    unnamed x0 -> x1, local copies, waits for them, and re-layouts: none -> 2.01 us
    pallas_call x1 -> x0, Pallas kernels: 1.74 us -> none  [on_device(): pl.pallas_call(table_kernel, out_shape=jax.ShapeDtypeStruct((TAB, 128), I...]
    pad x1 -> x0, local copies, waits for them, and re-layouts: 1.74 us -> none  [on_device(): kvn = jnp.pad(new_kv[0], ((0, 0), (0, NEWPAD - new_kv.shape[2]), (0, 0)))]
where the time goes in v3:
time: 96.4 us; the launch traced here: 96.2 us
  Pallas kernels  92.3 us (96%)
  local copies, waits for them, and re-layouts  3.2 us (3%)
    pallas_call x1, Pallas kernels, on_device(): pl.pallas_call(functools.partial(main_kernel, groups, lanes_tp), out_shap...  92.3 us
    unnamed x1, local copies, waits for them, and re-layouts  2.01 us

profile of v3, /device:TPU:1, one launch (start us, length us, event | category | flops | bytes accessed | tf_op | source)
XLA Modules:
  0.0 96.2 jit_solution(6832186414564061788)
XLA Ops:
  0.6 92.3 %shard_map.104 = (bf16[64,32,128]{2,1,0:T(8,128)(2,1)}, f32[8,128]{1,0:T(8,128)}) custom-call(s32[8,128]{1,0:T(8,128)} %bitcast.29, s32[8,128]{1,0:T(8,128)} %bitcast.30, s32[8,128]{1,0:T(8,128)} %bitcast.31, s32[1,64]{1,0:T(1,128)} %bitcast.33, f32[8,128]{1,0:T(8,128)} %bitcast.32, bf16[64,32,128]{2,1,0:T(8,128)(2,1)} %bitcast.26, ...), custom_call_target="tpu_custom_call" | custom-call | tf_op jit(solution)/shard_map/pallas_call | solution.py:463
  93.0 1.2 %slice_bitcast_fusion = f32[64]{0:T(128)} fusion(f32[8,128]{1,0:T(8,128)} %get-tuple-element.5), kind=kLoop, calls=%fused_computation | loop fusion | bytes 512 | tf_op jit(solution)/shard_map/squeeze | solution.py:497
  94.2 2.0 %copy.15 = bf16[1,64,4,1024]{3,2,1,0:T(4,128)(2,1)} copy(bf16[1,64,4,1024]{3,2,1,0:T(4,128)(2,1)} %bitcast.25) | data formatting | bytes 1048576

commit v4 on v3

--- a/solution.py
+++ b/solution.py
@@ -102,9 +102,9 @@
 
 
 def main_kernel(
-    groups, lanes_tp, pdev_ref, slot_ref, length_ref, pid_ref, w_ref, q_hbm, kvn_hbm, prompt_hbm, pages_hbm,
+    groups, lanes_tp, pdev_hbm, slot_hbm, length_hbm, pid_hbm, w_hbm, q_hbm, kvn_hbm, prompt_hbm, pages_hbm,
     out_ref, score_ref,
-    table, tab, q_ref, kvn_ref, pages, kv0, kv1, kv2, kv3, kv4, send, recv, ret_out, ret_in, stat_out, stat_in,
+    pdev_ref, slot_ref, length_ref, pid_ref, w_ref, table, tab, q_ref, kvn_ref, pages, kv0, kv1, kv2, kv3, kv4, send, recv, ret_out, ret_in, stat_out, stat_in,
     qt, kvt, acc, high, part, share, shares,
     q_ss, q_rs, r_ss, r_rs, s_ss, s_rs, f_ss, f_rs, b_ss, b_rs, x_ss, x_rs, c_ss, c_rs, l_sem,
 ):
@@ -140,8 +140,11 @@
     load_pages = pltpu.make_async_copy(pages_hbm, pages, l_sem.at[1])
     load_queries = pltpu.make_async_copy(q_hbm, q_ref, l_sem.at[3])
     load_new = pltpu.make_async_copy(kvn_hbm, kvn_ref, l_sem.at[4])
-    for load in (load_prompt, load_queries, load_new, load_pages):
-        load.start()
+    load_small = [
+        pltpu.make_async_copy(src, dst, l_sem.at[5 + i])
+        for i, (src, dst) in enumerate((
+            (pdev_hbm, pdev_ref), (slot_hbm, slot_ref), (length_hbm, length_ref), (pid_hbm, pid_ref), (w_hbm, w_ref)))]
+    load_prompt.start()
 
     barrier = pltpu.get_barrier_semaphore()
 
@@ -190,12 +193,16 @@
         src, dst = x_plan[i]
         return shard_copy(src, dst, side, x_ss.at[i], x_rs.at[i])
 
+    for load in load_small + [load_queries, load_new, load_pages]:
+        load.start()
     load_prompt.wait()
     pl.semaphore_wait(barrier, HOLD - 1 + groups - 1)
     fwd_copy(1).start()
     bwd_copy(1).start()
     x_copy(0).start()
 
+    for load in load_small:
+        load.wait()
     make_table(pdev_ref, slot_ref, length_ref, pid_ref, table)
     load_table = pltpu.make_async_copy(table, tab, l_sem.at[2])
     load_table.start()
@@ -355,14 +362,14 @@
     step_part(0, ret_in, stat_in)
     lax.fori_loop(0, TILES, new_part, 0)
     ring_step(1)
-    lax.fori_loop(5, 9, send_near, 0)
+    lax.fori_loop(5, 11, send_near, 0)
     ring_step(2)
-    lax.fori_loop(9, 15, send_near, 0)
+    lax.fori_loop(11, 15, send_near, 0)
     query_first(0)
+    ring_step(3)
     lax.fori_loop(1, 5, serve, 0)
-    ring_step(3)
+    ring_step(4)
     lax.fori_loop(5, 9, serve, 0)
-    ring_step(4)
     lax.fori_loop(9, 15, serve, 0)
     x_copy(0).wait_recv()
     prompt_part(0)
@@ -378,6 +385,15 @@
     x_copy(7).wait_recv()
     prompt_part(4)
 
+    def settle(t, _):
+        sums = acc[pl.ds(t * TILE, TILE)]
+        total = sums[:, :, HEAD:]
+        acc[pl.ds(t * TILE, TILE), :, :HEAD] = sums[:, :, :HEAD] / total
+        high[pl.ds(t * TILE, TILE)] = high[pl.ds(t * TILE, TILE)] + jnp.log2(total)
+        return 0
+
+    lax.fori_loop(0, TILES, settle, 0)
+
     def await_back(o, _):
         for copy in back_copy(o):
             copy.wait_recv()
@@ -393,46 +409,48 @@
         weights = jnp.where(head_of == j, w_ref[j:j + 1, :], weights)
 
     def finish(i, _):
-        for u in range(4):
-            b = i * 4 + u
+        for u in range(8):
+            b = i * 8 + u
             a = tab[ARRIVAL, b] & (HOLD * CAP - 1)
             place = jnp.clip(tab[PLACE, b], 0, PLACES - 1)
             line = stat_in[a >> 3, pl.ds((a >> 2) & 1, 1), :]
             level = jnp.sum(jnp.where(lane_of == (a & 3) * ROWS, line, 0.0), axis=1, keepdims=True)
-            old = high[place]
-            top = jnp.maximum(old, level)
-            mine, theirs = jnp.exp2(old - top), jnp.exp2(level - top)
-            sums = acc[place]
-            whole = sums[:, :HEAD] * mine + ret_in[a].astype(F32) * theirs
-            result = (whole / (sums[:, HEAD:] * mine + theirs)).astype(BF16)
+            mine = 1.0 / (1.0 + jnp.exp2(level - high[place]))
+            theirs = ret_in[a].astype(F32)
+            result = (theirs + (acc[place, :, :HEAD] - theirs) * mine).astype(BF16)
             out_ref[b] = result
             part[pl.ds(b, 1), :] = jnp.sum(result.astype(F32) * weights, axis=0, keepdims=True)
         return 0
 
-    lax.fori_loop(0, BEAMS // 4, finish, 0)
+    lax.fori_loop(0, BEAMS // 8, finish, 0)
 
     score = jnp.sum(part[...], axis=1, keepdims=True)
     spot = iota((BEAMS, 128), 0) == iota((BEAMS, 128), 1)
     line = jnp.sum(jnp.where(spot, score, 0.0), axis=0, keepdims=True) * 0.25
     share[...] = jnp.broadcast_to(line, (8, 128))
     if groups > 1:
-        def share_copy(o):
+        steps = [(g, h, y) for h in (1, 0) for y in (2, 1, 3, 0) for g in (1, 0) if (g, h, y) != (0, 0, 0)]
+        if (groups, lanes_tp) != (16, 8):
+            steps = None
+
+        def share_copy(i):
+            if steps is None:
+                to = group_peer(i)
+            else:
+                g, h, y = steps[i - 1]
+                to = {
+                    "grp": lax.rem(grp + g, 2),
+                    "tp": lax.rem(lax.div(tp, 4) + h, 2) * 4 + lax.rem(lax.rem(tp, 4) + y, 4)}
             return pltpu.make_async_remote_copy(
-                src_ref=share, dst_ref=shares.at[group], send_sem=c_ss.at[o], recv_sem=c_rs.at[o],
-                device_id=group_peer(o), device_id_type=MESH)
-
-        def send_share(o, _):
-            share_copy(o).start()
-            return 0
-
-        lax.fori_loop(1, groups, send_share, 0)
+                src_ref=share, dst_ref=shares.at[group], send_sem=c_ss.at[i], recv_sem=c_rs.at[i],
+                device_id=to, device_id_type=MESH)
+
+        share_copies = [share_copy(i) for i in range(1, groups)]
+        for copy in share_copies:
+            copy.start()
         shares[group] = share[...]
-
-        def await_share(o, _):
-            share_copy(o).wait()
-            return 0
-
-        lax.fori_loop(1, groups, await_share, 0)
+        for copy in share_copies:
+            copy.wait()
         score_ref[...] = jnp.sum(shares[...], axis=0)
     else:
         score_ref[...] = share[...]
@@ -466,9 +484,14 @@
             jax.ShapeDtypeStruct((BEAMS, ROWS, HEAD), BF16),
             jax.ShapeDtypeStruct((8, 128), F32),
         ),
-        in_specs=[vmem] * 5 + [hbm] * 4,
+        in_specs=[hbm] * 9,
         out_specs=(vmem, vmem),
         scratch_shapes=[
+            pltpu.VMEM((8, 128), I32),
+            pltpu.VMEM((8, 128), I32),
+            pltpu.VMEM((8, 128), I32),
+            pltpu.VMEM((1, BEAMS), I32),
+            pltpu.VMEM((8, HEAD), F32),
             pltpu.VMEM((TAB, 128), I32),
             pltpu.SMEM((TAB, 128), I32),
             pltpu.VMEM((BEAMS, ROWS, HEAD), BF16),
@@ -488,7 +511,7 @@
             pltpu.VMEM((BEAMS, 128), F32),
             pltpu.VMEM((8, 128), F32),
             pltpu.VMEM((max(groups, 1), 8, 128), F32),
-        ] + [dma((HOLD,))] * 6 + [dma((5,))] * 4 + [dma((8,))] * 2 + [dma((max(groups, 1),))] * 2 + [dma((5,))],
+        ] + [dma((HOLD,))] * 6 + [dma((5,))] * 4 + [dma((8,))] * 2 + [dma((max(groups, 1),))] * 2 + [dma((10,))],
         compiler_params=pltpu.CompilerParams(
             collective_id=0, has_side_effects=True, vmem_limit_bytes=VMEM_LIMIT),
     )(parent_dev.reshape(8, 128), parent_slot.reshape(8, 128), cache_len.reshape(8, 128), prompt_ids.reshape(1, BEAMS),

time: 96.4 us -> 95.4 us (0.990)
  no operation moved by 1% of the time
where the time goes in v4:
time: 95.4 us; the launch traced here: 95.2 us
  Pallas kernels  91.4 us (96%)
  local copies, waits for them, and re-layouts  3.2 us (3%)
    pallas_call x1, Pallas kernels, on_device(): pl.pallas_call(functools.partial(main_kernel, groups, lanes_tp), out_shap...  91.4 us
    unnamed x1, local copies, waits for them, and re-layouts  2.01 us

profile of v4, /device:TPU:1, one launch (start us, length us, event | category | flops | bytes accessed | tf_op | source)
XLA Modules:
  0.0 95.2 jit_solution(14167306494363451702)
XLA Ops:
  0.6 91.4 %shard_map.104 = (bf16[64,32,128]{2,1,0:T(8,128)(2,1)}, f32[8,128]{1,0:T(8,128)}) custom-call(s32[8,128]{1,0:T(8,128)} %bitcast.29, s32[8,128]{1,0:T(8,128)} %bitcast.30, s32[8,128]{1,0:T(8,128)} %bitcast.31, s32[1,64]{1,0:T(1,128)} %bitcast.33, f32[8,128]{1,0:T(8,128)} %bitcast.32, bf16[64,32,128]{2,1,0:T(8,128)(2,1)} %bitcast.26, ...), custom_call_target="tpu_custom_call" | custom-call | tf_op jit(solution)/shard_map/pallas_call | solution.py:481
  92.0 1.2 %slice_bitcast_fusion = f32[64]{0:T(128)} fusion(f32[8,128]{1,0:T(8,128)} %get-tuple-element.5), kind=kLoop, calls=%fused_computation | loop fusion | bytes 512 | tf_op jit(solution)/shard_map/squeeze | solution.py:520
  93.2 2.0 %copy.15 = bf16[1,64,4,1024]{3,2,1,0:T(4,128)(2,1)} copy(bf16[1,64,4,1024]{3,2,1,0:T(4,128)(2,1)} %bitcast.25) | data formatting | bytes 1048576

commit v5 on v4

--- a/solution.py
+++ b/solution.py
@@ -193,6 +193,9 @@
         src, dst = x_plan[i]
         return shard_copy(src, dst, side, x_ss.at[i], x_rs.at[i])
 
+    def x_last(half):
+        return shard_copy(ANTI, XANTI, side, x_ss.at[7 + half], x_rs.at[7 + half], half)
+
     for load in load_small + [load_queries, load_new, load_pages]:
         load.start()
     load_prompt.wait()
@@ -239,12 +242,14 @@
         if s < 4:
             fwd_copy(s + 1).start()
             x_copy(2 * s - 1).start()
+        else:
+            x_last(0).start()
         bwd_copy(s).wait_recv()
         if s < 4:
             bwd_copy(s + 1).start()
             x_copy(2 * s).start()
         else:
-            x_copy(7).start()
+            x_last(1).start()
 
     def fill_tile(t, _):
         for i in range(TILE):
@@ -382,7 +387,8 @@
     for i in (5, 6):
         x_copy(i).wait_recv()
     prompt_part(3)
-    x_copy(7).wait_recv()
+    for half in (0, 1):
+        x_last(half).wait_recv()
     prompt_part(4)
 
     def settle(t, _):
@@ -465,8 +471,10 @@
     for s in (1, 2, 3, 4):
         fwd_copy(s).wait_send()
         bwd_copy(s).wait_send()
-    for i in range(8):
+    for i in range(7):
         x_copy(i).wait_send()
+    for half in (0, 1):
+        x_last(half).wait_send()
 
 
 def on_device(queries, new_kv, prompt_key_value, step_key_value, parent_dev, parent_slot, cache_len, prompt_ids, score_weights):
@@ -511,7 +519,7 @@
             pltpu.VMEM((BEAMS, 128), F32),
             pltpu.VMEM((8, 128), F32),
             pltpu.VMEM((max(groups, 1), 8, 128), F32),
-        ] + [dma((HOLD,))] * 6 + [dma((5,))] * 4 + [dma((8,))] * 2 + [dma((max(groups, 1),))] * 2 + [dma((10,))],
+        ] + [dma((HOLD,))] * 6 + [dma((5,))] * 4 + [dma((9,))] * 2 + [dma((max(groups, 1),))] * 2 + [dma((10,))],
         compiler_params=pltpu.CompilerParams(
             collective_id=0, has_side_effects=True, vmem_limit_bytes=VMEM_LIMIT),
     )(parent_dev.reshape(8, 128), parent_slot.reshape(8, 128), cache_len.reshape(8, 128), prompt_ids.reshape(1, BEAMS),

time: 95.4 us -> 95.4 us (level)
  no operation moved by 1% of the time
where the time goes in v5:
time: 95.4 us; the launch traced here: 95.2 us
  Pallas kernels  91.4 us (96%)
  local copies, waits for them, and re-layouts  3.2 us (3%)
    pallas_call x1, Pallas kernels, on_device(): pl.pallas_call(functools.partial(main_kernel, groups, lanes_tp), out_shap...  91.4 us
    unnamed x1, local copies, waits for them, and re-layouts  2.01 us

profile of v5, /device:TPU:1, one launch (start us, length us, event | category | flops | bytes accessed | tf_op | source)
XLA Modules:
  0.0 95.2 jit_solution(10263255851736502483)
XLA Ops:
  0.6 91.4 %shard_map.104 = (bf16[64,32,128]{2,1,0:T(8,128)(2,1)}, f32[8,128]{1,0:T(8,128)}) custom-call(s32[8,128]{1,0:T(8,128)} %bitcast.29, s32[8,128]{1,0:T(8,128)} %bitcast.30, s32[8,128]{1,0:T(8,128)} %bitcast.31, s32[1,64]{1,0:T(1,128)} %bitcast.33, f32[8,128]{1,0:T(8,128)} %bitcast.32, bf16[64,32,128]{2,1,0:T(8,128)(2,1)} %bitcast.26, ...), custom_call_target="tpu_custom_call" | custom-call | tf_op jit(solution)/shard_map/pallas_call | solution.py:489
  92.0 1.2 %slice_bitcast_fusion = f32[64]{0:T(128)} fusion(f32[8,128]{1,0:T(8,128)} %get-tuple-element.5), kind=kLoop, calls=%fused_computation | loop fusion | bytes 512 | tf_op jit(solution)/shard_map/squeeze | solution.py:528
  93.2 2.0 %copy.15 = bf16[1,64,4,1024]{3,2,1,0:T(4,128)(2,1)} copy(bf16[1,64,4,1024]{3,2,1,0:T(4,128)(2,1)} %bitcast.25) | data formatting | bytes 1048576
